TPU v7x, 32 devices: a whole 2x2x4 slice. The times are simulated.
32 devices in a mesh: shard: 2 (over z_hi), ctx: 8 (over y, x, core), tensor: 2 (over z_lo).
Axes of the slice: x: 2, y: 2, z: 4 (z_hi: 2, z_lo: 2; z = z_hi * 2 + z_lo), core: 2. Of those that a mesh axis runs over, the one named last changes fastest.
Arguments:
- tokens: bfloat16 [16384, 1024], P(('shard', 'ctx')), may hold values from -6 to 6
- cont_lengths: int32 [2, 8], P('shard'), may hold values from 1 to 1024, 4096 in all within a row
- attn_gain: bfloat16 [1024], P(('shard', 'ctx')), may hold values from 0.099609375 to 1.8984375
- ffn_gain: bfloat16 [1024], P(('shard', 'ctx')), may hold values from 0.099609375 to 1.8984375
- query_gain: bfloat16 [128], P(('shard', 'ctx')), may hold values from 0.5 to 1.59375
- key_gain: bfloat16 [128], P(('shard', 'ctx')), may hold values from 0.5 to 1.59375
- w_query: bfloat16 [1024, 2048], P(('shard', 'ctx'), 'tensor'), may hold values from -0.1875 to 0.1875
- key_weight: bfloat16 [1024, 1024], P(('shard', 'ctx'), 'tensor'), may hold values from -0.1875 to 0.1875
- value_weight: bfloat16 [1024, 1024], P(('shard', 'ctx'), 'tensor'), may hold values from -0.1875 to 0.1875
- w_out: bfloat16 [2048, 1024], P('tensor', ('shard', 'ctx')), may hold values from -1.5 to 1.5
- w_gate: bfloat16 [1024, 3072], P(('shard', 'ctx'), 'tensor'), may hold values from -0.1875 to 0.1875
- w_up: bfloat16 [1024, 3072], P(('shard', 'ctx'), 'tensor'), may hold values from -0.1875 to 0.1875
- w_down: bfloat16 [3072, 1024], P('tensor', ('shard', 'ctx')), may hold values from -0.109375 to 0.109375
- cotangent: bfloat16 [16384, 1024], P(('shard', 'ctx')), may hold values from -6 to 6
Outputs:
- layer_out: bfloat16 [16384, 1024], P(('shard', 'ctx'))
- grad_tokens: bfloat16 [16384, 1024], P(('shard', 'ctx'))
- grad_attn_gain: float32 [1024], P(('shard', 'ctx'))
- grad_ffn_gain: float32 [1024], P(('shard', 'ctx'))
- grad_query_gain: float32 [128], P(('shard', 'ctx'))
- grad_key_gain: float32 [128], P(('shard', 'ctx'))
- grad_w_query: float32 [1024, 2048], P(('shard', 'ctx'), 'tensor')
- grad_w_key: float32 [1024, 1024], P(('shard', 'ctx'), 'tensor')
- grad_w_value: float32 [1024, 1024], P(('shard', 'ctx'), 'tensor')
- grad_w_out: float32 [2048, 1024], P('tensor', ('shard', 'ctx'))
- grad_w_gate: float32 [1024, 3072], P(('shard', 'ctx'), 'tensor')
- grad_w_up: float32 [1024, 3072], P(('shard', 'ctx'), 'tensor')
- grad_w_down: float32 [3072, 1024], P('tensor', ('shard', 'ctx'))
Inputs may be any that keep to these rules, and one draw needn't show every extreme that they name: `cont_lengths`: each row holds the lengths of one group's 8 continuations, summing to 4096, the largest exactly 1024.
All inputs are finite; a program needn't handle non-finite values.
Results may differ from a plain program's by a relative error of at most 0.019.
Values may be sent and summed in bfloat16 or wider, within the bound.
No kernel may reach another device: no remote copies, remote signals or barrier semaphores. Data moves between devices by JAX's collectives and lax.ppermute only.
A program may use at most 640 MiB of HBM per device.

v0:
```python
import math

import jax
import jax.numpy as jnp
from jax import lax
from jax.sharding import PartitionSpec as P

HEAD_SIZE = 128
PROMPT = 4096
CONT_TOK = 4096


EPSILON = 1e-06
ROPE_BASE = 1000000.0
MASKED = -1e30


def token_tags(row_ids, lengths, prompt_dev, cont_dev, prompt_len):
    per_dev = prompt_dev + cont_dev
    device = row_ids // per_dev
    offset = row_ids - device * per_dev
    is_prompt = offset < prompt_dev
    cont_at = device * cont_dev + offset - prompt_dev
    cont_ends = jnp.cumsum(lengths)
    seg_num = jnp.sum((cont_ends[None, :] <= cont_at[:, None]).astype(jnp.int32), axis=1)
    starts = cont_ends - lengths
    slots = jnp.arange(lengths.shape[0], dtype=jnp.int32)
    picked = jnp.sum(jnp.where(slots[None, :] == seg_num[:, None], starts[None, :], 0), axis=1)
    position = jnp.where(is_prompt, device * prompt_dev + offset, prompt_len + cont_at - picked)
    segment = jnp.where(is_prompt, -1, seg_num)
    return (segment, position)


def visible(seg_query, pos_query, seg_key, pos_key):
    causal = pos_key[None, :] <= pos_query[:, None]
    same = (seg_key[None, :] < 0) | (seg_key[None, :] == seg_query[:, None])
    return causal & same


def root_mean_gain(values, gain_vec):
    return (
        values * lax.rsqrt(jnp.mean(values * values, axis=-1, keepdims=True) + EPSILON) * gain_vec
    )


def rotary(head_values, position):
    half_dim = head_values.shape[-1] // 2
    inverse_freq = jnp.exp(
        jnp.arange(half_dim, dtype=jnp.float32) * (-math.log(ROPE_BASE) / half_dim)
    )
    angles = position.astype(jnp.float32)[:, None] * inverse_freq[None, :]
    cosine = jnp.concatenate([jnp.cos(angles), jnp.cos(angles)], axis=-1)[:, None, :]
    sine_table = jnp.concatenate([jnp.sin(angles), jnp.sin(angles)], axis=-1)[:, None, :]
    rotated = jnp.concatenate([-head_values[..., half_dim:], head_values[..., :half_dim]], axis=-1)
    return head_values * cosine + rotated * sine_table


def swiglu(gate_in, up_in):
    return jax.nn.silu(gate_in) * up_in


def body(
    tokens,
    cont_lengths,
    attn_gain,
    ffn_gain,
    query_gain,
    key_gain,
    w_query,
    key_weight,
    value_weight,
    w_out,
    w_gate,
    w_up,
    w_down,
    cotangent,
):
    ctx_size = lax.axis_size("ctx")
    prompt_dev = PROMPT // ctx_size
    cont_dev = CONT_TOK // ctx_size
    per_dev = tokens.shape[0]
    group_rows = per_dev * ctx_size
    lengths = cont_lengths[0]
    local_rows = lax.axis_index("ctx") * per_dev + jnp.arange(per_dev, dtype=jnp.int32)
    seg_query, pos_query = token_tags(local_rows, lengths, prompt_dev, cont_dev, PROMPT)
    seg_keys_all, pos_keys_all = token_tags(
        jnp.arange(group_rows, dtype=jnp.int32), lengths, prompt_dev, cont_dev, PROMPT
    )
    shard_step = math.gcd(ctx_size, max(1, 512 // per_dev))
    block_rows = shard_step * per_dev
    blocks = ctx_size // shard_step
    score_scale = 1.0 / math.sqrt(HEAD_SIZE)
    gathered = (
        lax.all_gather(attn_gain, ("shard", "ctx"), axis=0, tiled=True),
        lax.all_gather(ffn_gain, ("shard", "ctx"), axis=0, tiled=True),
        lax.all_gather(query_gain, ("shard", "ctx"), axis=0, tiled=True),
        lax.all_gather(key_gain, ("shard", "ctx"), axis=0, tiled=True),
        lax.all_gather(w_query, ("shard", "ctx"), axis=0, tiled=True),
        lax.all_gather(key_weight, ("shard", "ctx"), axis=0, tiled=True),
        lax.all_gather(value_weight, ("shard", "ctx"), axis=0, tiled=True),
        lax.all_gather(w_out, ("shard", "ctx"), axis=1, tiled=True),
        lax.all_gather(w_gate, ("shard", "ctx"), axis=0, tiled=True),
        lax.all_gather(w_up, ("shard", "ctx"), axis=0, tiled=True),
        lax.all_gather(w_down, ("shard", "ctx"), axis=1, tiled=True),
    )
    full_attn_gain, full_ffn_gain, full_query_gain, full_key_gain = (
        gathered[0],
        gathered[1],
        gathered[2],
        gathered[3],
    )
    full_query, full_key, full_value, full_out = (
        gathered[4],
        gathered[5],
        gathered[6],
        gathered[7],
    )
    full_gate, full_up, full_down = (gathered[8], gathered[9], gathered[10])

    def local_chain(linear, gain_vec):
        return rotary(root_mean_gain(linear.reshape(per_dev, -1, HEAD_SIZE), gain_vec), pos_query)

    inputs = tokens.astype(jnp.float32)
    normed_f, norm_one_back = jax.vjp(root_mean_gain, inputs, full_attn_gain.astype(jnp.float32))
    normed = normed_f.astype(jnp.bfloat16)
    q_linear = jnp.dot(normed, full_query, preferred_element_type=jnp.float32)
    k_linear = jnp.dot(normed, full_key, preferred_element_type=jnp.float32)
    v_linear = jnp.dot(normed, full_value, preferred_element_type=jnp.float32)
    query_f, query_back = jax.vjp(local_chain, q_linear, full_query_gain.astype(jnp.float32))
    key_f, key_back = jax.vjp(local_chain, k_linear, full_key_gain.astype(jnp.float32))
    kv_heads = key_f.shape[1]
    group_size = query_f.shape[1] // kv_heads
    queries = query_f.astype(jnp.bfloat16).reshape(per_dev, kv_heads, group_size, HEAD_SIZE)
    keys_local = key_f.astype(jnp.bfloat16).reshape(per_dev, kv_heads * HEAD_SIZE)
    values_local = v_linear.astype(jnp.bfloat16)
    key_block = lax.all_gather(keys_local, "ctx", axis=0, tiled=True)
    run_max = jnp.full((per_dev, kv_heads, group_size), MASKED, jnp.float32)
    key_count = key_block.shape[0]
    seg_key = seg_keys_all
    pos_key = pos_keys_all
    allowed = visible(seg_query, pos_query, seg_key, pos_key)[:, None, None, :]
    key_heads = key_block.reshape(key_count, kv_heads, HEAD_SIZE)
    value_heads = lax.all_gather(values_local, "ctx", axis=0, tiled=True).reshape(
        key_count, kv_heads, HEAD_SIZE
    )
    scores = (
        jnp.einsum("rkgd,nkd->rkgn", queries, key_heads, preferred_element_type=jnp.float32)
        * score_scale
    )
    scores = jnp.where(allowed, scores, MASKED)
    new_max = jnp.maximum(run_max, jnp.max(scores, axis=-1))
    weights_now = jnp.where(allowed, jnp.exp(scores - new_max[..., None]), 0.0)
    run_sum = jnp.sum(weights_now, axis=-1)
    run_acc = jnp.einsum(
        "rkgn,nkd->rkgd",
        weights_now.astype(jnp.bfloat16),
        value_heads,
        preferred_element_type=jnp.float32,
    )
    final_state = (new_max, run_sum, run_acc)
    run_max, run_sum, run_acc = final_state
    attended = run_acc / run_sum[..., None]
    log_total = run_max + jnp.log(run_sum)
    attended_low = attended.reshape(per_dev, -1).astype(jnp.bfloat16)
    attn_part = jnp.dot(attended_low, full_out, preferred_element_type=jnp.float32)
    residual = inputs + lax.psum(attn_part.astype(jnp.bfloat16), "tensor").astype(jnp.float32)
    normed_ffn_f, norm_two_back = jax.vjp(
        root_mean_gain, residual, full_ffn_gain.astype(jnp.float32)
    )
    normed_ffn = normed_ffn_f.astype(jnp.bfloat16)
    gate_proj = jnp.dot(normed_ffn, full_gate, preferred_element_type=jnp.float32)
    up_proj = jnp.dot(normed_ffn, full_up, preferred_element_type=jnp.float32)
    hidden_f, swiglu_back = jax.vjp(swiglu, gate_proj, up_proj)
    hidden = hidden_f.astype(jnp.bfloat16)
    down_part = jnp.dot(hidden, full_down, preferred_element_type=jnp.float32)
    layer_out = (
        residual + lax.psum(down_part.astype(jnp.bfloat16), "tensor").astype(jnp.float32)
    ).astype(jnp.bfloat16)
    again = (
        lax.all_gather(attn_gain, ("shard", "ctx"), axis=0, tiled=True),
        lax.all_gather(ffn_gain, ("shard", "ctx"), axis=0, tiled=True),
        lax.all_gather(query_gain, ("shard", "ctx"), axis=0, tiled=True),
        lax.all_gather(key_gain, ("shard", "ctx"), axis=0, tiled=True),
        lax.all_gather(w_query, ("shard", "ctx"), axis=0, tiled=True),
        lax.all_gather(key_weight, ("shard", "ctx"), axis=0, tiled=True),
        lax.all_gather(value_weight, ("shard", "ctx"), axis=0, tiled=True),
        lax.all_gather(w_out, ("shard", "ctx"), axis=1, tiled=True),
        lax.all_gather(w_gate, ("shard", "ctx"), axis=0, tiled=True),
        lax.all_gather(w_up, ("shard", "ctx"), axis=0, tiled=True),
        lax.all_gather(w_down, ("shard", "ctx"), axis=1, tiled=True),
    )
    back_query, back_key, back_value, back_out = (again[4], again[5], again[6], again[7])
    back_gate, back_up, back_down = (again[8], again[9], again[10])
    back_keys, back_values = (
        lax.all_gather(keys_local, "ctx", axis=0, tiled=True),
        lax.all_gather(values_local, "ctx", axis=0, tiled=True),
    )
    grad_down_local = jnp.einsum("rf,rd->fd", hidden, cotangent, preferred_element_type=jnp.float32)
    grad_hidden = jnp.einsum("rd,fd->rf", cotangent, back_down, preferred_element_type=jnp.float32)
    grad_gate_f, grad_up_f = swiglu_back(grad_hidden)
    grad_gate = grad_gate_f.astype(jnp.bfloat16)
    grad_upper = grad_up_f.astype(jnp.bfloat16)
    grad_gate_local = jnp.einsum(
        "rd,rf->df", normed_ffn, grad_gate, preferred_element_type=jnp.float32
    )
    grad_up_local = jnp.einsum(
        "rd,rf->df", normed_ffn, grad_upper, preferred_element_type=jnp.float32
    )
    ffn_back_part = jnp.einsum(
        "rf,df->rd", grad_gate, back_gate, preferred_element_type=jnp.float32
    ) + jnp.einsum("rf,df->rd", grad_upper, back_up, preferred_element_type=jnp.float32)
    grad_normed_ffn = lax.psum(ffn_back_part.astype(jnp.bfloat16), "tensor").astype(jnp.float32)
    grad_resid_norm, grad_ffn_gain_local = norm_two_back(grad_normed_ffn)
    grad_resid = cotangent.astype(jnp.float32) + grad_resid_norm
    grad_mixed = grad_resid.astype(jnp.bfloat16)
    grad_out_local = jnp.einsum(
        "rh,rd->hd", attended_low, grad_mixed, preferred_element_type=jnp.float32
    )
    grad_attended = jnp.einsum(
        "rd,hd->rh", grad_mixed, back_out, preferred_element_type=jnp.float32
    )
    grad_attended = grad_attended.astype(jnp.bfloat16).reshape(
        per_dev, kv_heads, group_size, HEAD_SIZE
    )
    row_delta = jnp.sum(grad_attended.astype(jnp.float32) * attended, axis=-1)

    def backward_block(grad_query, block_index):
        key_start = block_index * block_rows
        key_block = lax.dynamic_slice_in_dim(back_keys, key_start, block_rows, 0).reshape(
            block_rows, kv_heads, HEAD_SIZE
        )
        value_block = lax.dynamic_slice_in_dim(back_values, key_start, block_rows, 0).reshape(
            block_rows, kv_heads, HEAD_SIZE
        )
        seg_key = lax.dynamic_slice_in_dim(seg_keys_all, key_start, block_rows, 0)
        pos_key = lax.dynamic_slice_in_dim(pos_keys_all, key_start, block_rows, 0)
        allowed = visible(seg_query, pos_query, seg_key, pos_key)[:, None, None, :]
        scores = (
            jnp.einsum("rkgd,nkd->rkgn", queries, key_block, preferred_element_type=jnp.float32)
            * score_scale
        )
        scores = jnp.where(allowed, scores, MASKED)
        probabilities = jnp.where(allowed, jnp.exp(scores - log_total[..., None]), 0.0)
        grad_value = jnp.einsum(
            "rkgn,rkgd->nkd",
            probabilities.astype(jnp.bfloat16),
            grad_attended,
            preferred_element_type=jnp.float32,
        )
        grad_probs = jnp.einsum(
            "rkgd,nkd->rkgn", grad_attended, value_block, preferred_element_type=jnp.float32
        )
        grad_scores = (probabilities * (grad_probs - row_delta[..., None])).astype(jnp.bfloat16)
        grad_query = grad_query + score_scale * jnp.einsum(
            "rkgn,nkd->rkgd", grad_scores, key_block, preferred_element_type=jnp.float32
        )
        grad_key = score_scale * jnp.einsum(
            "rkgn,rkgd->nkd", grad_scores, queries, preferred_element_type=jnp.float32
        )
        return (
            grad_query,
            (
                grad_key.reshape(block_rows, kv_heads * HEAD_SIZE),
                grad_value.reshape(block_rows, kv_heads * HEAD_SIZE),
            ),
        )

    grad_query, key_value_grads = lax.scan(
        backward_block,
        jnp.zeros((per_dev, kv_heads, group_size, HEAD_SIZE), jnp.float32),
        jnp.arange(blocks, dtype=jnp.int32),
    )
    feature = kv_heads * HEAD_SIZE
    grad_key_all = key_value_grads[0].reshape(-1, feature)
    grad_value_all = key_value_grads[1].reshape(-1, feature)
    own_key_gradient, grad_value_own = (
        lax.psum_scatter(
            grad_key_all.astype(jnp.bfloat16), "ctx", scatter_dimension=0, tiled=True
        ).astype(jnp.float32),
        lax.psum_scatter(
            grad_value_all.astype(jnp.bfloat16), "ctx", scatter_dimension=0, tiled=True
        ).astype(jnp.float32),
    )
    grad_q_linear, grad_query_gain_part = query_back(
        grad_query.reshape(per_dev, kv_heads * group_size, HEAD_SIZE)
    )
    grad_k_linear, grad_key_gain_part = key_back(
        own_key_gradient.reshape(per_dev, kv_heads, HEAD_SIZE)
    )
    grad_q_low = grad_q_linear.astype(jnp.bfloat16)
    grad_k_low = grad_k_linear.astype(jnp.bfloat16)
    grad_v_low = grad_value_own.astype(jnp.bfloat16)
    grad_query_local = jnp.einsum(
        "rd,rh->dh", normed, grad_q_low, preferred_element_type=jnp.float32
    )
    grad_key_local = jnp.einsum("rd,rh->dh", normed, grad_k_low, preferred_element_type=jnp.float32)
    grad_value_local = jnp.einsum(
        "rd,rh->dh", normed, grad_v_low, preferred_element_type=jnp.float32
    )
    attn_back_part = (
        jnp.einsum("rh,dh->rd", grad_q_low, back_query, preferred_element_type=jnp.float32)
        + jnp.einsum("rh,dh->rd", grad_k_low, back_key, preferred_element_type=jnp.float32)
        + jnp.einsum("rh,dh->rd", grad_v_low, back_value, preferred_element_type=jnp.float32)
    )
    grad_normed, grad_query_gain_sum, grad_key_gain_sum = (
        lax.psum(attn_back_part.astype(jnp.bfloat16), "tensor").astype(jnp.float32),
        lax.psum(grad_query_gain_part.astype(jnp.bfloat16), "tensor").astype(jnp.float32),
        lax.psum(grad_key_gain_part.astype(jnp.bfloat16), "tensor").astype(jnp.float32),
    )
    grad_inputs_norm, grad_attn_gain_local = norm_one_back(grad_normed)
    grad_tokens = (grad_resid + grad_inputs_norm).astype(jnp.bfloat16)
    shares = (
        lax.psum_scatter(grad_attn_gain_local, ("shard", "ctx"), scatter_dimension=0, tiled=True),
        lax.psum_scatter(grad_ffn_gain_local, ("shard", "ctx"), scatter_dimension=0, tiled=True),
        lax.psum_scatter(grad_query_gain_sum, ("shard", "ctx"), scatter_dimension=0, tiled=True),
        lax.psum_scatter(grad_key_gain_sum, ("shard", "ctx"), scatter_dimension=0, tiled=True),
        lax.psum_scatter(grad_query_local, ("shard", "ctx"), scatter_dimension=0, tiled=True),
        lax.psum_scatter(grad_key_local, ("shard", "ctx"), scatter_dimension=0, tiled=True),
        lax.psum_scatter(grad_value_local, ("shard", "ctx"), scatter_dimension=0, tiled=True),
        lax.psum_scatter(grad_out_local, ("shard", "ctx"), scatter_dimension=1, tiled=True),
        lax.psum_scatter(grad_gate_local, ("shard", "ctx"), scatter_dimension=0, tiled=True),
        lax.psum_scatter(grad_up_local, ("shard", "ctx"), scatter_dimension=0, tiled=True),
        lax.psum_scatter(grad_down_local, ("shard", "ctx"), scatter_dimension=1, tiled=True),
    )
    return (
        layer_out,
        grad_tokens,
        shares[0],
        shares[1],
        shares[2],
        shares[3],
        shares[4],
        shares[5],
        shares[6],
        shares[7],
        shares[8],
        shares[9],
        shares[10],
    )


def solution(mesh):
    in_specs = (
        P(("shard", "ctx"), None),
        P("shard", None),
        P(("shard", "ctx")),
        P(("shard", "ctx")),
        P(("shard", "ctx")),
        P(("shard", "ctx")),
        P(("shard", "ctx"), "tensor"),
        P(("shard", "ctx"), "tensor"),
        P(("shard", "ctx"), "tensor"),
        P("tensor", ("shard", "ctx")),
        P(("shard", "ctx"), "tensor"),
        P(("shard", "ctx"), "tensor"),
        P("tensor", ("shard", "ctx")),
        P(("shard", "ctx"), None),
    )
    out_specs = (
        P(("shard", "ctx"), None),
        P(("shard", "ctx"), None),
        P(("shard", "ctx")),
        P(("shard", "ctx")),
        P(("shard", "ctx")),
        P(("shard", "ctx")),
        P(("shard", "ctx"), "tensor"),
        P(("shard", "ctx"), "tensor"),
        P(("shard", "ctx"), "tensor"),
        P("tensor", ("shard", "ctx")),
        P(("shard", "ctx"), "tensor"),
        P(("shard", "ctx"), "tensor"),
        P("tensor", ("shard", "ctx")),
    )
    return jax.shard_map(body, mesh=mesh, in_specs=in_specs, out_specs=out_specs, check_vma=False)
```

profile of v0, /device:TPU:0, one launch (start us, length us, event | category | flops | bytes accessed | tf_op | source)
XLA Modules:
  0.0 2340.6 jit_solution(10683169670679912254)
XLA Ops:
  15.5 36.7 %all-reduce.13 = (bf16[1024]{0:T(1024)(128)(2,1)S(1)}, bf16[128]{0:T(256)(128)(2,1)S(1)}, bf16[128]{0:T(256)(128)(2,1)S(1)}, bf16[1024]{0:T(1024)(128)(2,1)}) all-reduce(bf16[1024]{0:T(1024)(128)(2,1)S(1)} %dynamic-update-slice, bf16[128]{0:T(256)(128)(2,1)S(1)} %dynamic-update-slice.1, ...), channel_id=1, replica_groups=mesh['shard'=2,'ctx'=8,'tensor'=2] {'shard','ctx'}, use_global_device_ids=true, to_apply=%add.4 | all-reduce | flops 2304 | bytes 9216
  63.7 21.4 all-gather.10.cloned.1.call-done
  102.3 25.8 %all-gather.18.cloned.1.call-done = bf16[1024,1024]{1,0:T(8,128)(2,1)} async-done(((bf16[64,1024]{1,0:T(8,128)(2,1)}), bf16[1024,1024]{1,0:T(8,128)(2,1)}) %all-gather.18.cloned.1.call-update) | async-done | bytes 2097168 | tf_op jit(solution)/shard_map/all_gather | solution.py:98
  142.2 41.7 %all-gather.16.cloned.1.call-done = bf16[8192,512]{0,1:T(8,128)(2,1)} async-done(((bf16[1024,512]{0,1:T(8,128)(2,1)}), bf16[8192,512]{0,1:T(8,128)(2,1)}) %all-gather.16.cloned.1.call-update) | async-done | bytes 8388624 | tf_op jit(solution)/shard_map/all_gather | solution.py:136
  183.9 98.1 %fusion.12 = (f32[1024,4,2]{0,2,1:T(2,128)S(1)}, f32[4,8192,1024,2]{2,1,3,0:T(8,128)}) fusion(pred[1024,8192]{0,1:T(8,128)(4,1)} %or_and_fusion.1, bf16[8192,4,128,1]{0,2,3,1:T(8,128)(2,1)} %bitcast.231, bf16[1024,4,2,128]{0,3,2,1:T(8,128)(2,1)S(1)} %fusion.37), kind=kOutput, calls=%fused_computation.23 | convolution fusion | flops 17381187584 | bytes 287342592 | tf_op jit(solution)/shard_map/rkgd,nkd->rkgn/dot_general | solution.py:147
  282.6 83.4 %fusion.13 = f32[1024,4,2]{0,2,1:T(2,128)S(1)} fusion(f32[4,8192,1024,2]{2,1,3,0:T(8,128)} %get-tuple-element.283, f32[1024,4,2]{0,2,1:T(2,128)S(1)} %broadcast_maximum_fusion, pred[1024,8192]{0,1:T(8,128)(4,1)} %or_and_fusion.1), kind=kLoop, calls=%fused_computation.24 | loop fusion | flops 335536128 | bytes 276889600 | tf_op jit(solution)/shard_map/reduce_sum | solution.py:153
  378.0 92.1 %fusion.88 = (bf16[1024,4,2,128]{0,3,2,1:T(8,128)(2,1)}, f32[1024,4,2,128]{0,3,2,1:T(8,128)}) fusion(f32[1024,4,2]{0,2,1:T(2,128)S(1)} %fusion.13, bf16[8192,4,128,1]{0,2,3,1:T(8,128)(2,1)} %bitcast.225, f32[4,8192,1024,2]{2,1,3,0:T(8,128)} %get-tuple-element.283, f32[1024,4,2]{0,2,1:T(2,128)S(1)} %broadcast_maximum_fusion, ...), kind=kOutput, calls=%fused_computation.177 | convolution fusion | flops 17517510656 | bytes 291569664 | tf_op jit(solution)/shard_map/rkgn,nkd->rkgd/dot_general | solution.py:154
  478.4 61.7 %all-reduce.20.cloned.1.call-done = bf16[1024,1024]{1,0:T(8,128)(2,1)} async-done(((bf16[1024,1024]{1,0:T(8,128)(2,1)}), bf16[1024,1024]{1,0:T(8,128)(2,1)}) %all-reduce.20.cloned.1.call-update) | async-done | bytes 2097168 | tf_op jit(solution)/shard_map/psum | solution.py:166
  544.7 46.3 %all-gather.22.cloned.1.call-done = bf16[1024,1536]{1,0:T(8,128)(2,1)} async-done(((bf16[64,1536]{1,0:T(8,128)(2,1)}), bf16[1024,1536]{1,0:T(8,128)(2,1)}) %all-gather.22.cloned.1.call-update) | async-done | bytes 3145744 | tf_op jit(solution)/shard_map/all_gather | solution.py:102
  599.5 41.3 %all-gather.24.cloned.1.call-done = bf16[1024,1536]{1,0:T(8,128)(2,1)} async-done(((bf16[64,1536]{1,0:T(8,128)(2,1)}), bf16[1024,1536]{1,0:T(8,128)(2,1)}) %all-gather.24.cloned.1.call-update) | async-done | bytes 3145744 | tf_op jit(solution)/shard_map/all_gather | solution.py:103
  649.4 41.1 %all-gather.26.cloned.1.call-done = bf16[1536,1024]{0,1:T(8,128)(2,1)} async-done(((bf16[1536,64]{0,1:T(8,128)(2,1)}), bf16[1536,1024]{0,1:T(8,128)(2,1)}) %all-gather.26.cloned.1.call-update) | async-done | bytes 3145744 | tf_op jit(solution)/shard_map/all_gather | solution.py:104
  711.4 62.5 %all-reduce.22.cloned.1.call-done = bf16[1024,1024]{1,0:T(8,128)(2,1)} async-done(((bf16[1024,1024]{1,0:T(8,128)(2,1)}), bf16[1024,1024]{1,0:T(8,128)(2,1)}) %all-reduce.22.cloned.1.call-update) | async-done | bytes 2097168 | tf_op jit(solution)/shard_map/psum | solution.py:212
  786.7 703.4 %while.15 = (s32[]{:T(128)}, f32[1024,4,2,128]{0,3,2,1:T(8,128)}, bf16[8,1024,512]{2,1,0:T(8,128)(2,1)}, bf16[8,1024,512]{2,1,0:T(8,128)(2,1)}, s32[8]{0:T(128)S...) while((s32[]{:T(128)}, f32[1024,4,2,128]{0,3,2,1:T(8,128)}, ...), condition=%wide.region_17.18_spmd.clone, body=%wide.region_16.17_spmd.clone.sunk | while | flops 10846471168 | bytes 201460560 | solution.py:268
  792.8 13.2 fusion.167
  807.3 21.6 fusion.168
  841.3 16.9 fusion.169
  879.6 13.2 fusion.167
  894.1 21.6 fusion.168
  928.1 16.9 fusion.169
  967.6 13.2 fusion.167
  982.1 21.6 fusion.168
  1016.1 16.9 fusion.169
  1055.6 13.2 fusion.167
  1070.1 21.6 fusion.168
  1104.1 16.9 fusion.169
  1143.6 13.2 fusion.167
  1158.1 21.6 fusion.168
  1192.1 16.9 fusion.169
  1231.6 13.2 fusion.167
  1246.1 21.6 fusion.168
  1280.1 16.9 fusion.169
  1319.6 13.2 fusion.167
  1334.1 21.6 fusion.168
  1368.2 16.9 fusion.169
  1407.6 13.2 fusion.167
  1422.1 21.6 fusion.168
  1456.2 16.9 fusion.169
  1512.4 49.2 %reduce-scatter.10.cloned.1.call-done = bf16[1024,512]{1,0:T(8,128)(2,1)} async-done(((bf16[8192,512]{1,0:T(8,128)(2,1)}), bf16[1024,512]{1,0:T(8,128)(2,1)}) %reduce-scatter.10.cloned.1.call-update) | async-done | bytes 1048592 | tf_op jit(solution)/shard_map/reduce_scatter | solution.py:277
  1570.9 65.8 %reduce-scatter.12.cloned.1.call-done = bf16[1024,512]{1,0:T(8,128)(2,1)} async-done(((bf16[8192,512]{1,0:T(8,128)(2,1)}), bf16[1024,512]{1,0:T(8,128)(2,1)}) %reduce-scatter.12.cloned.1.call-update) | async-done | bytes 1048592 | tf_op jit(solution)/shard_map/reduce_scatter | solution.py:280
  1699.6 52.5 %all-reduce.24.cloned.1.call-done = (bf16[1024,1024]{1,0:T(8,128)(2,1)}, bf16[1024,1024]{1,0:T(8,128)(2,1)}) async-done(((bf16[1024,1024]{1,0:T(8,128)(2,1)}, bf16[1024,1024]{1,0:T(8,128)(2,1)}), (bf16[1024,1024]{1,0:T(8,128)(2,1)}, bf16[1024,1024]{1,0:T(8,128)(2,1)})) %all-reduce.24.cloned.1.call-update) | async-done | bytes 4194320 | tf_op jit(solution)/shard_map/psum | solution.py:177
  1755.4 67.8 %all-reduce.12 = (f32[1024]{0:T(1024)S(1)}, f32[1024]{0:T(1024)S(1)}, f32[128]{0:T(128)S(1)}, f32[128]{0:T(128)S(1)}) all-reduce(f32[1024]{0:T(1024)S(1)} %get-tuple-element.207, f32[1024]{0:T(1024)S(1)} %copy-done.53, bf16[128]{0:T(256)(128)(2,1)S(1)} %get-tuple-element.249, ...), channel_id=4, replica_groups=mesh['shard'=2,'ctx'=8,'tensor'=2] {'shard','ctx'}, use_global_device_ids=true, to_apply=%region_25.26.clone | all-reduce | flops 2304 | bytes 17920
  1832.9 20.4 reduce-scatter.24.cloned.1.call-done
  1853.3 99.3 %reduce-scatter.22.cloned.1.call-done = f32[64,1536]{1,0:T(8,128)} async-done(((f32[1024,1536]{1,0:T(8,128)}), f32[64,1536]{1,0:T(8,128)}) %reduce-scatter.22.cloned.1.call-update) | async-done | bytes 393232 | tf_op jit(solution)/shard_map/reduce_scatter | solution.py:321
  1952.6 99.9 %reduce-scatter.26.cloned.1.call-done = f32[1536,64]{0,1:T(8,128)} async-done(((f32[1536,1024]{0,1:T(8,128)}), f32[1536,64]{0,1:T(8,128)}) %reduce-scatter.26.cloned.1.call-update) | async-done | bytes 393232 | tf_op jit(solution)/shard_map/reduce_scatter | solution.py:323
  2052.5 73.8 %reduce-scatter.20.cloned.1.call-done = f32[1024,64]{0,1:T(8,128)} async-done(((f32[1024,1024]{0,1:T(8,128)}), f32[1024,64]{0,1:T(8,128)}) %reduce-scatter.20.cloned.1.call-update) | async-done | bytes 262160 | tf_op jit(solution)/shard_map/reduce_scatter | solution.py:320
  2126.3 72.8 %reduce-scatter.14.cloned.1.call-done = f32[64,1024]{1,0:T(8,128)} async-done(((f32[1024,1024]{1,0:T(8,128)}), f32[64,1024]{1,0:T(8,128)}) %reduce-scatter.14.cloned.1.call-update) | async-done | bytes 262160 | tf_op jit(solution)/shard_map/reduce_scatter | solution.py:317
  2199.2 66.8 %reduce-scatter.16.cloned.1.call-done = f32[64,512]{1,0:T(8,128)} async-done(((f32[1024,512]{1,0:T(8,128)}), f32[64,512]{1,0:T(8,128)}) %reduce-scatter.16.cloned.1.call-update) | async-done | bytes 131088 | tf_op jit(solution)/shard_map/reduce_scatter | solution.py:318
  2265.9 67.4 %reduce-scatter.18.cloned.1.call-done = f32[64,512]{1,0:T(8,128)} async-done(((f32[1024,512]{1,0:T(8,128)}), f32[64,512]{1,0:T(8,128)}) %reduce-scatter.18.cloned.1.call-update) | async-done | bytes 131088 | tf_op jit(solution)/shard_map/reduce_scatter | solution.py:319
  (388 shorter events, 515.4 us)
Async XLA Ops:
  7.2 51.0 %copy-start.5 = (bf16[1024,1024]{1,0:T(8,128)(2,1)S(1)}, bf16[1024,1024]{1,0:T(8,128)(2,1)}, u32[]{:S(2)}) copy-start(bf16[1024,1024]{1,0:T(8,128)(2,1)} %param.16) | copy-start | bytes 6291460
  7.2 51.0 %all-gather.14.cloned.1.call-start = ((), (), s32[]{:S(2)}) async-start(), calls=%async_computation.11 | async-start | bytes 1114112 | tf_op jit(solution)/shard_map/all_gather | solution.py:99
  7.9 77.2 %all-gather.10.cloned.1.call-start = ((), (), s32[]{:S(2)}) async-start(), calls=%async_computation.9 | async-start | bytes 1114112 | tf_op jit(solution)/shard_map/all_gather | solution.py:100
  8.7 119.4 %all-gather.18.cloned.1.call-start = ((), (), s32[]{:S(2)}) async-start(), calls=%async_computation.13 | async-start | bytes 2228224 | tf_op jit(solution)/shard_map/all_gather | solution.py:98
  9.4 174.4 %all-gather.16.cloned.1.call-start = ((), (), s32[]{:S(2)}) async-start(), calls=%async_computation.12 | async-start | bytes 9437184 | tf_op jit(solution)/shard_map/all_gather | solution.py:136
  52.2 75.9 %copy-start.47 = (f32[1024]{0:T(1024)}, f32[1024]{0:T(1024)S(1)}, u32[]{:S(2)}) copy-start(f32[1024]{0:T(1024)S(1)} %convert_element_type.152) | copy-start | bytes 12292
  54.0 35.9 %copy-start.31 = (s32[1024]{0:T(1024)}, s32[1024]{0:T(1024)S(1)}, u32[]{:S(2)}) copy-start(s32[1024]{0:T(1024)S(1)} %get-tuple-element.396) | copy-start | bytes 12292
  55.1 83.7 %copy-start.14 = (f32[1024,128]{0,1:T(8,128)}, f32[1024,128]{0,1:T(8,128)S(1)}, u32[]{:S(2)}) copy-start(f32[1024,128]{0,1:T(8,128)S(1)} %get-tuple-element.289) | copy-start | bytes 1572868
  55.1 83.7 %copy-start.16 = (f32[1024,128]{0,1:T(8,128)}, f32[1024,128]{0,1:T(8,128)S(1)}, u32[]{:S(2)}) copy-start(f32[1024,128]{0,1:T(8,128)S(1)} %get-tuple-element.288) | copy-start | bytes 1572868
  58.2 70.0 %copy-start.49 = (f32[1024]{0:T(1024)}, f32[1024]{0:T(1024)S(1)}, u32[]{:S(2)}) copy-start(f32[1024]{0:T(1024)S(1)} %fusion.62) | copy-start | bytes 12292
  63.7 302.3 %all-gather.12.cloned.1.call-start = ((), (), s32[]{:S(2)}) async-start(), calls=%async_computation.10 | async-start | bytes 9437184 | tf_op jit(solution)/shard_map/all_gather | solution.py:143
  88.6 381.6 %all-gather.20.cloned.1.call-start = ((), (), s32[]{:S(2)}) async-start(), calls=%async_computation.14 | async-start | bytes 2228224 | tf_op jit(solution)/shard_map/all_gather | solution.py:101
  89.2 450.9 %all-reduce.20.cloned.1.call-start = ((), (), s32[]{:S(2)}) async-start(), calls=%async_computation.15 | async-start | bytes 4194304 | tf_op jit(solution)/shard_map/psum | solution.py:166
  89.9 49.0 %copy-start.56 = (f32[128]{0:T(128)}, f32[128]{0:T(128)S(1)}, u32[]{:S(2)}) copy-start(f32[128]{0:T(128)S(1)} %convert_element_type.160) | copy-start | bytes 1540
  142.2 139.8 %copy-start = (bf16[1024,4,2,128]{0,3,2,1:T(8,128)(2,1)}, bf16[1024,4,2,128]{0,3,2,1:T(8,128)(2,1)S(1)}, u32[]{:S(2)}) copy-start(bf16[1024,4,2,128]{0,3,2,1:T(8,128)(2,1)S(1)} %fusion.37) | copy-start | bytes 6291460
  470.2 69.9 %copy-start.6 = (bf16[1024,1024]{1,0:T(8,128)(2,1)S(1)}, bf16[1024,1024]{1,0:T(8,128)(2,1)}, u32[]{:S(2)}) copy-start(bf16[1024,1024]{1,0:T(8,128)(2,1)} %param.16) | copy-start | bytes 6291460
  476.3 114.7 %all-gather.22.cloned.1.call-start = ((), (), s32[]{:S(2)}) async-start(), calls=%async_computation.16 | async-start | bytes 3342336 | tf_op jit(solution)/shard_map/all_gather | solution.py:102
  477.0 163.8 %all-gather.24.cloned.1.call-start = ((), (), s32[]{:S(2)}) async-start(), calls=%async_computation.17 | async-start | bytes 3342336 | tf_op jit(solution)/shard_map/all_gather | solution.py:103
  477.8 212.8 %all-gather.26.cloned.1.call-start = ((), (), s32[]{:S(2)}) async-start(), calls=%async_computation.18 | async-start | bytes 3342336 | tf_op jit(solution)/shard_map/all_gather | solution.py:104
  478.3 295.6 %all-reduce.22.cloned.1.call-start = ((), (), s32[]{:S(2)}) async-start(), calls=%async_computation.19 | async-start | bytes 4194304 | tf_op jit(solution)/shard_map/psum | solution.py:212
  478.4 300.2 %copy-start.39 = (f32[1024]{0:T(1024)}, f32[1024]{0:T(1024)S(1)}, u32[]{:S(2)}) copy-start(f32[1024]{0:T(1024)S(1)} %convert_element_type.167) | copy-start | bytes 12292
  542.6 236.0 %copy-start.41 = (f32[1024]{0:T(1024)}, f32[1024]{0:T(1024)S(1)}, u32[]{:S(2)}) copy-start(f32[1024]{0:T(1024)S(1)} %fusion.63) | copy-start | bytes 12292
  711.2 850.3 %reduce-scatter.10.cloned.1.call-start = ((), (), s32[]{:S(2)}) async-start(), calls=%async_computation.20 | async-start | bytes 9437184 | tf_op jit(solution)/shard_map/reduce_scatter | solution.py:277
  791.1 16.2 copy-start.13
  792.8 14.5 copy-start.63
  877.9 16.2 copy-start.13
  879.6 14.5 copy-start.63
  965.9 16.2 copy-start.13
  967.6 14.5 copy-start.63
  1053.9 16.2 copy-start.13
  1055.6 14.5 copy-start.63
  1141.9 16.2 copy-start.13
  1143.6 14.5 copy-start.63
  1229.9 16.2 copy-start.13
  1317.9 16.2 copy-start.13
  1405.9 16.2 copy-start.13
  1490.1 146.6 %reduce-scatter.12.cloned.1.call-start = ((), (), s32[]{:S(2)}) async-start(), calls=%async_computation.21 | async-start | bytes 9437184 | tf_op jit(solution)/shard_map/reduce_scatter | solution.py:280
  1490.9 261.2 %all-reduce.24.cloned.1.call-start = ((), (), s32[]{:S(2)}) async-start(), calls=%async_computation.29 | async-start | bytes 8388608 | tf_op jit(solution)/shard_map/psum | solution.py:177
  1567.6 69.1 %copy-start.22 = (bf16[1024,512]{1,0:T(8,128)(2,1)S(1)}, bf16[1024,512]{1,0:T(8,128)(2,1)}, u32[]{:S(2)}) copy-start(bf16[1024,512]{1,0:T(8,128)(2,1)} %all-gather.10.cloned.1.call-done) | copy-start | bytes 3145732
  1643.1 210.2 %reduce-scatter.24.cloned.1.call-start = ((), (), s32[]{:S(2)}) async-start(), calls=%async_computation.27 | async-start | bytes 6684672 | tf_op jit(solution)/shard_map/reduce_scatter | solution.py:322
  1651.9 300.7 %reduce-scatter.22.cloned.1.call-start = ((), (), s32[]{:S(2)}) async-start(), calls=%async_computation.26 | async-start | bytes 6684672 | tf_op jit(solution)/shard_map/reduce_scatter | solution.py:321
  1659.6 393.0 %reduce-scatter.26.cloned.1.call-start = ((), (), s32[]{:S(2)}) async-start(), calls=%async_computation.28 | async-start | bytes 6684672 | tf_op jit(solution)/shard_map/reduce_scatter | solution.py:323
  1668.4 457.9 %reduce-scatter.20.cloned.1.call-start = ((), (), s32[]{:S(2)}) async-start(), calls=%async_computation.25 | async-start | bytes 4456448 | tf_op jit(solution)/shard_map/reduce_scatter | solution.py:320
  1678.9 520.3 %reduce-scatter.14.cloned.1.call-start = ((), (), s32[]{:S(2)}) async-start(), calls=%async_computation.22 | async-start | bytes 4456448 | tf_op jit(solution)/shard_map/reduce_scatter | solution.py:317
  1685.9 580.0 %reduce-scatter.16.cloned.1.call-start = ((), (), s32[]{:S(2)}) async-start(), calls=%async_computation.23 | async-start | bytes 2228224 | tf_op jit(solution)/shard_map/reduce_scatter | solution.py:318
  1690.3 643.0 %reduce-scatter.18.cloned.1.call-start = ((), (), s32[]{:S(2)}) async-start(), calls=%async_computation.24 | async-start | bytes 2228224 | tf_op jit(solution)/shard_map/reduce_scatter | solution.py:319
  1693.1 62.3 %copy-start.53 = (f32[1024]{0:T(1024)S(1)}, f32[1024]{0:T(1024)}, u32[]{:S(2)}) copy-start(f32[1024]{0:T(1024)} %get-tuple-element.203) | copy-start | bytes 12292
  1693.1 132.5 %copy-start.46 = (f32[1024]{0:T(1024)S(1)}, f32[1024]{0:T(1024)}, u32[]{:S(2)}) copy-start(f32[1024]{0:T(1024)} %copy-done.45) | copy-start | bytes 12292
  (53 other events, 208.9 us)
Sparse Core Ops, SparseCore 0:
  10.3 38.2 all-gather.13
  51.0 34.0 all-gather.9
  87.4 40.6 all-gather.17
  130.4 53.3 all-gather.15
  186.2 54.3 all-gather.11
  242.8 41.6 all-gather.19
  476.4 63.6 all-reduce.19
  542.6 48.2 all-gather.21
  593.5 47.2 all-gather.23
  643.2 47.2 all-gather.25
  711.4 62.5 all-reduce.21
  1490.2 71.2 reduce-scatter.9
  1565.4 71.2 reduce-scatter.11
  1643.2 108.8 all-reduce.23
  1757.6 95.7 reduce-scatter.23
  1858.2 94.3 reduce-scatter.21
  1958.1 94.3 reduce-scatter.25
  2055.2 71.0 reduce-scatter.19
  2129.2 69.9 reduce-scatter.13
  2201.9 64.0 reduce-scatter.15
  2268.8 64.4 reduce-scatter.17
where the time goes:
time: 2350 us; the launch traced here: 2340 us
  waiting for transfers between devices  1010 us (43%)
  matrix products  906 us (39%)
  other arithmetic  152 us (6%)
  local copies, waits for them, and re-layouts  132 us (6%)
  blocking collectives  110 us (5%)
    dot_general x8, matrix products, backward_block(): jnp.einsum('rkgd,nkd->rkgn', grad_attended, value_block, preferred_elemen...  173 us
    dot_general x8, matrix products, backward_block(): jnp.einsum('rkgn,rkgd->nkd', probabilities.astype(jnp.bfloat16), grad_att...  135 us
    dot_general x8, matrix products, backward_block(): jnp.einsum('rkgd,nkd->rkgn', queries, key_block, preferred_element_type=j...  105 us
    unnamed x2, blocking collectives  105 us
    reduce_scatter x1, waiting for transfers between devices, body(): lax.psum_scatter(grad_down_local, ('shard', 'ctx'), scatter_dimension=1,...  99.9 us
    reduce_scatter x1, waiting for transfers between devices, body(): lax.psum_scatter(grad_gate_local, ('shard', 'ctx'), scatter_dimension=0,...  99.3 us
    dot_general x1, matrix products, body(): jnp.einsum('rkgd,nkd->rkgn', queries, key_heads, preferred_element_type=j...  98.1 us
    dot_general x1, matrix products, body(): jnp.einsum('rkgn,nkd->rkgd', weights_now.astype(jnp.bfloat16), value_head...  92.1 us
  transfers between devices with their start and end apart: 21, of which 18 were waited for; matrix products, arithmetic and copies ran while one was open for 18% of the time, Pallas kernels for 0%

commit v1 on v0

v1 whole, which is shorter than its diff:
```python
import functools
import math

import jax
import jax.numpy as jnp
from jax import lax
from jax.experimental import pallas as pl
from jax.experimental.pallas import tpu as pltpu
from jax.sharding import PartitionSpec as P

HEAD_SIZE = 128
PROMPT = 4096
CONT_TOK = 4096
LONGEST = 1024

EPSILON = 1e-06
ROPE_BASE = 1000000.0
MASKED = -1e30
LOG2E = math.log2(math.e)
LN2 = math.log(2.0)

BF = jnp.bfloat16
F32 = jnp.float32
NN = (((1,), (0,)), ((), ()))
NT = (((1,), (1,)), ((), ()))
TN = (((0,), (0,)), ((), ()))


def mm(left, right, dims=NN):
    return lax.dot_general(left, right, dims, preferred_element_type=F32)


def fwd_kernel(n_slots, n_halo, prompt, cont, idx_ref, q_ref, lo_ref, *refs):
    k_slots, refs = refs[:n_slots], refs[n_slots:]
    v_slots, refs = refs[:n_slots], refs[n_slots:]
    k_halo, refs = refs[:n_halo], refs[n_halo:]
    v_halo, refs = refs[:n_halo], refs[n_halo:]
    out_ref, lse_ref, acc, tot = refs
    me, lo_first = idx_ref[0], idx_ref[1]

    def fold(weights):
        part = weights[:, :128]
        for at in range(128, weights.shape[1], 128):
            part = part + weights[:, at : at + 128]
        return part

    def attend(g, rows, start, k_ref, v_ref, mask=None):
        scores = mm(q_ref[start : start + rows, g * 128 : (g + 1) * 128], k_ref[...], NT)
        if mask is not None:
            scores = jnp.where(mask, scores, MASKED)
        weights = jnp.exp2(scores)
        return mm(weights.astype(BF), v_ref[...]), fold(weights)

    def add(g, rows, start, k_ref, v_ref, mask=None):
        part, total = attend(g, rows, start, k_ref, v_ref, mask)
        acc[g, start : start + rows, :] += part
        tot[g, start : start + rows, :] += total

    row = lax.broadcasted_iota(jnp.int32, (prompt, 1), 0)
    col = lax.broadcasted_iota(jnp.int32, (1, prompt), 1)
    for g in range(2):
        part, total = attend(g, prompt, 0, k_slots[0], v_slots[0], col <= row)
        acc[g, :prompt, :] = part
        tot[g, :prompt, :] = total
    low = lo_ref[:, :1]
    row = lax.broadcasted_iota(jnp.int32, (cont, 1), 0)
    col = lax.broadcasted_iota(jnp.int32, (1, cont), 1)
    mask = (col <= row) & (col >= low)
    for g in range(2):
        part, total = attend(g, cont, prompt, k_halo[0], v_halo[0], mask)
        acc[g, prompt:, :] = part
        tot[g, prompt:, :] = total
    for d in range(1, n_halo):

        @pl.when(lo_first < -(d - 1) * cont)
        def _(d=d):
            for g in range(2):
                add(g, cont, prompt, k_halo[d], v_halo[d], col - d * cont >= low)

    for s in range(1, n_slots):

        @pl.when(jnp.bitwise_xor(me, s) < me)
        def _(s=s):
            for g in range(2):
                add(g, prompt, 0, k_slots[s], v_slots[s])

    for s in range(n_slots):
        for g in range(2):
            add(g, cont, prompt, k_slots[s], v_slots[s])
    for g in range(2):
        total = jnp.sum(tot[g], axis=1, keepdims=True)
        out_ref[:, g * 128 : (g + 1) * 128] = acc[g] / total
        lse_ref[0, g : g + 1, :] = jnp.log2(jnp.sum(tot[g].T, axis=0, keepdims=True))


def attention_forward(me, lo_first, q, low_col, k_slots, v_slots, k_halo, v_halo, prompt, cont):
    rows = q.shape[0]
    heads = k_slots[0].shape[1] // HEAD_SIZE
    n_slots, n_halo = len(k_slots), len(k_halo)
    wide = pl.BlockSpec((rows, 256), lambda h, i: (0, h))
    slot = pl.BlockSpec((prompt, 128), lambda h, i: (0, h))
    halo = pl.BlockSpec((cont, 128), lambda h, i: (0, h))
    low = pl.BlockSpec((cont, 128), lambda h, i: (0, 0))
    pairs = heads * 2 * (rows * prompt * n_slots + cont * cont * n_halo)
    return pl.pallas_call(
        functools.partial(fwd_kernel, n_slots, n_halo, prompt, cont),
        grid_spec=pltpu.PrefetchScalarGridSpec(
            num_scalar_prefetch=1,
            grid=(heads,),
            in_specs=[wide, low] + [slot] * (2 * n_slots) + [halo] * (2 * n_halo),
            out_specs=[wide, pl.BlockSpec((1, 8, rows), lambda h, i: (h, 0, 0))],
            scratch_shapes=[pltpu.VMEM((2, rows, 128), F32), pltpu.VMEM((2, rows, 128), F32)],
        ),
        out_shape=[
            jax.ShapeDtypeStruct((rows, heads * 256), F32),
            jax.ShapeDtypeStruct((heads, 8, rows), F32),
        ],
        compiler_params=pltpu.CompilerParams(vmem_limit_bytes=48 * 2**20),
        cost_estimate=pl.CostEstimate(
            flops=pairs * 512, bytes_accessed=24 * 2**20, transcendentals=pairs
        ),
        name="attention_forward",
    )(jnp.stack([me, lo_first]), q, low_col, *k_slots, *v_slots, *k_halo, *v_halo)


def bwd_kernel(n_slots, n_halo, prompt, cont, idx_ref, q_ref, do_ref, o_ref, lse_ref, lo_ref, *refs):
    k_slots, refs = refs[:n_slots], refs[n_slots:]
    v_slots, refs = refs[:n_slots], refs[n_slots:]
    k_halo, refs = refs[:n_halo], refs[n_halo:]
    v_halo, refs = refs[:n_halo], refs[n_halo:]
    dq_ref, refs = refs[0], refs[1:]
    dk_slots, refs = refs[:n_slots], refs[n_slots:]
    dv_slots, refs = refs[:n_slots], refs[n_slots:]
    dk_halo, refs = refs[:n_halo], refs[n_halo:]
    dv_halo, refs = refs[:n_halo], refs[n_halo:]
    qp, qc, dop, doc, lsep, lsec, delp, delc, dqp, dqc, dk_acc, dv_acc = refs
    me, lo_first = idx_ref[0], idx_ref[1]
    for g in range(2):
        cols = slice(g * 128, (g + 1) * 128)
        at_p, at_c = slice(g * prompt, (g + 1) * prompt), slice(g * cont, (g + 1) * cont)
        qp[at_p, :] = q_ref[:prompt, cols]
        qc[at_c, :] = q_ref[prompt:, cols]
        dop[at_p, :] = do_ref[:prompt, cols]
        doc[at_c, :] = do_ref[prompt:, cols]
        lsep[:, at_p] = lse_ref[0, g : g + 1, :prompt]
        lsec[:, at_c] = lse_ref[0, g : g + 1, prompt:]
        delta = jnp.sum((do_ref[:, cols].astype(F32) * o_ref[:, cols]).T, axis=0, keepdims=True)
        delp[:, at_p] = delta[:, :prompt]
        delc[:, at_c] = delta[:, prompt:]
    dqp[...] = jnp.zeros_like(dqp)
    dqc[...] = jnp.zeros_like(dqc)

    def block(k_ref, v_ref, q, do, lse, delta, dq, mask=None):
        keys = k_ref[...]
        scores = mm(keys, q[...], NT)
        dp = mm(v_ref[...], do[...], NT)
        scores = scores - lse[...]
        if mask is not None:
            scores = jnp.where(mask, scores, MASKED)
        probs = jnp.exp2(scores)
        ds = (probs * (dp - delta[...])).astype(BF)
        dq[...] += mm(keys.T, ds)
        return mm(ds, q[...]), mm(probs.astype(BF), do[...])

    prompt_side = (qp, dop, lsep, delp, dqp)
    cont_side = (qc, doc, lsec, delc, dqc)

    lane = lax.broadcasted_iota(jnp.int32, (1, 2 * cont), 1)
    lane = jnp.where(lane >= cont, lane - cont, lane)
    key = lax.broadcasted_iota(jnp.int32, (cont, 1), 0)
    low = lo_ref[:1, :]
    dk, dv = block(k_halo[0], v_halo[0], *cont_side, (key <= lane) & (key >= low))
    dk_halo[0][...] = (dk * LN2).astype(BF)
    dv_halo[0][...] = dv.astype(BF)
    for d in range(1, n_halo):
        needed = lo_first < -(d - 1) * cont

        @pl.when(needed)
        def _(d=d):
            dk, dv = block(k_halo[d], v_halo[d], *cont_side, key - d * cont >= low)
            dk_halo[d][...] = (dk * LN2).astype(BF)
            dv_halo[d][...] = dv.astype(BF)

        @pl.when(jnp.logical_not(needed))
        def _(d=d):
            dk_halo[d][...] = jnp.zeros_like(dk_halo[d])
            dv_halo[d][...] = jnp.zeros_like(dv_halo[d])

    lane = lax.broadcasted_iota(jnp.int32, (1, 2 * prompt), 1)
    lane = jnp.where(lane >= prompt, lane - prompt, lane)
    key = lax.broadcasted_iota(jnp.int32, (prompt, 1), 0)
    for s in range(n_slots):
        dk, dv = block(k_slots[s], v_slots[s], *cont_side)
        dk_acc[...] = dk
        dv_acc[...] = dv
        if s == 0:
            dk, dv = block(k_slots[s], v_slots[s], *prompt_side, key <= lane)
            dk_acc[...] += dk
            dv_acc[...] += dv
        else:

            @pl.when(jnp.bitwise_xor(me, s) < me)
            def _(s=s):
                dk, dv = block(k_slots[s], v_slots[s], *prompt_side)
                dk_acc[...] += dk
                dv_acc[...] += dv

        dk_slots[s][...] = (dk_acc[...] * LN2).astype(BF)
        dv_slots[s][...] = dv_acc[...].astype(BF)
    scale = 1.0 / math.sqrt(HEAD_SIZE)
    for g in range(2):
        cols = slice(g * 128, (g + 1) * 128)
        dq_ref[:prompt, cols] = dqp[:, g * prompt : (g + 1) * prompt].T * scale
        dq_ref[prompt:, cols] = dqc[:, g * cont : (g + 1) * cont].T * scale


def attention_backward(
    me, lo_first, q, do, out, lse, low_row, k_slots, v_slots, k_halo, v_halo, prompt, cont
):
    rows = q.shape[0]
    heads = k_slots[0].shape[1] // HEAD_SIZE
    n_slots, n_halo = len(k_slots), len(k_halo)
    wide = pl.BlockSpec((rows, 256), lambda h, i: (0, h))
    slot = pl.BlockSpec((prompt, 128), lambda h, i: (0, h))
    halo = pl.BlockSpec((cont, 128), lambda h, i: (0, h))
    low = pl.BlockSpec((8, 2 * cont), lambda h, i: (0, 0))
    pairs = heads * 2 * (rows * prompt * n_slots + cont * cont * n_halo)
    results = pl.pallas_call(
        functools.partial(bwd_kernel, n_slots, n_halo, prompt, cont),
        grid_spec=pltpu.PrefetchScalarGridSpec(
            num_scalar_prefetch=1,
            grid=(heads,),
            in_specs=[wide, wide, wide, pl.BlockSpec((1, 8, rows), lambda h, i: (h, 0, 0)), low]
            + [slot] * (2 * n_slots)
            + [halo] * (2 * n_halo),
            out_specs=[wide] + [slot] * (2 * n_slots) + [halo] * (2 * n_halo),
            scratch_shapes=[
                pltpu.VMEM((2 * prompt, 128), BF),
                pltpu.VMEM((2 * cont, 128), BF),
                pltpu.VMEM((2 * prompt, 128), BF),
                pltpu.VMEM((2 * cont, 128), BF),
                pltpu.VMEM((1, 2 * prompt), F32),
                pltpu.VMEM((1, 2 * cont), F32),
                pltpu.VMEM((1, 2 * prompt), F32),
                pltpu.VMEM((1, 2 * cont), F32),
                pltpu.VMEM((128, 2 * prompt), F32),
                pltpu.VMEM((128, 2 * cont), F32),
                pltpu.VMEM((prompt, 128), F32),
                pltpu.VMEM((prompt, 128), F32),
            ],
        ),
        out_shape=[jax.ShapeDtypeStruct((rows, heads * 256), F32)]
        + [jax.ShapeDtypeStruct((prompt, heads * 128), BF)] * (2 * n_slots)
        + [jax.ShapeDtypeStruct((cont, heads * 128), BF)] * (2 * n_halo),
        compiler_params=pltpu.CompilerParams(vmem_limit_bytes=52 * 2**20),
        cost_estimate=pl.CostEstimate(
            flops=pairs * 1280, bytes_accessed=40 * 2**20, transcendentals=pairs
        ),
        name="attention_backward",
    )(jnp.stack([me, lo_first]), q, do, out, lse, low_row, *k_slots, *v_slots, *k_halo, *v_halo)
    dq, results = results[0], results[1:]
    dk_slots, results = results[:n_slots], results[n_slots:]
    dv_slots, results = results[:n_slots], results[n_slots:]
    return dq, dk_slots, dv_slots, results[:n_halo], results[n_halo:]


def swap(value, axis, bit):
    size = lax.axis_size(axis)
    return lax.ppermute(value, axis, [(i, i ^ bit) for i in range(size)])


def add_low(left, right):
    return (left.astype(F32) + right.astype(F32)).astype(BF)


def gather_slots(keys, values):
    size = lax.axis_size("ctx")
    if size != 8:
        both = jnp.stack([keys, values])[None]
        bit = 1
        while bit < size:
            both = jnp.concatenate([both, swap(both, "ctx", bit)])
            bit *= 2
        return [both[s, 0] for s in range(size)], [both[s, 1] for s in range(size)]
    k, v = [None] * 8, [None] * 8
    k[0], v[0] = keys, values
    k[2], v[2] = swap(keys, "ctx", 2), swap(values, "ctx", 2)
    k[4], v[4] = swap(keys, "ctx", 4), swap(values, "ctx", 4)
    k[6], v[6] = swap(k[4], "ctx", 2), swap(v[2], "ctx", 4)
    for s in (0, 2, 4, 6):
        k[s + 1], v[s + 1] = swap(k[s], "ctx", 1), swap(v[s], "ctx", 1)
    return k, v


def scatter_slots(k, v):
    size = lax.axis_size("ctx")
    if size != 8:
        both = jnp.stack([jnp.stack(k), jnp.stack(v)], axis=1)
        while both.shape[0] > 1:
            half = both.shape[0] // 2
            both = add_low(both[:half], swap(both[half:], "ctx", half))
        return both[0, 0], both[0, 1]
    k, v = list(k), list(v)
    for s in (6, 4, 2, 0):
        k[s] = add_low(k[s], swap(k[s + 1], "ctx", 1))
        v[s] = add_low(v[s], swap(v[s + 1], "ctx", 1))
    k[4] = add_low(k[4], swap(k[6], "ctx", 2))
    v[2] = add_low(v[2], swap(v[6], "ctx", 4))
    k2, v2 = swap(k[2], "ctx", 2), swap(v[2], "ctx", 2)
    k4, v4 = swap(k[4], "ctx", 4), swap(v[4], "ctx", 4)
    dk = k[0].astype(F32) + k2.astype(F32) + k4.astype(F32)
    dv = v[0].astype(F32) + v2.astype(F32) + v4.astype(F32)
    return dk, dv


def shift(value, by):
    size = lax.axis_size("ctx")
    return lax.ppermute(value, "ctx", [(i, i + by) for i in range(size) if 0 <= i + by < size])


def exchange(part):
    low = part.astype(BF)
    return low.astype(F32) + swap(low, "tensor", 1).astype(F32)


def butterfly(value, axes):
    for axis in axes:
        bit = 1
        while bit < lax.axis_size(axis):
            value = value + swap(value, axis, bit)
            bit *= 2
    return value


def root_mean_gain(values, gain_vec):
    return (
        values * lax.rsqrt(jnp.mean(values * values, axis=-1, keepdims=True) + EPSILON) * gain_vec
    )


def rotary_tables(position):
    half_dim = HEAD_SIZE // 2
    inverse_freq = jnp.exp(
        jnp.arange(half_dim, dtype=F32) * (-math.log(ROPE_BASE) / half_dim)
    )
    angles = position.astype(F32)[:, None] * inverse_freq[None, :]
    cosine, sine = jnp.cos(angles), jnp.sin(angles)
    return (
        jnp.concatenate([cosine, cosine], axis=-1)[:, None, :],
        jnp.concatenate([sine, sine], axis=-1)[:, None, :],
    )


def rotary(head_values, tables):
    cosine, sine = tables
    half_dim = head_values.shape[-1] // 2
    rotated = jnp.concatenate([-head_values[..., half_dim:], head_values[..., :half_dim]], axis=-1)
    return head_values * cosine + rotated * sine


def swiglu(gate_in, up_in):
    return jax.nn.silu(gate_in) * up_in


def body(
    tokens,
    cont_lengths,
    attn_gain,
    ffn_gain,
    query_gain,
    key_gain,
    w_query,
    key_weight,
    value_weight,
    w_out,
    w_gate,
    w_up,
    w_down,
    cotangent,
):
    ctx_size = lax.axis_size("ctx")
    weight_axes = ("shard", "ctx")
    parts = lax.axis_size("shard") * ctx_size
    me = lax.axis_index("ctx")
    part = lax.axis_index("shard") * ctx_size + me
    prompt_dev = PROMPT // ctx_size
    cont_dev = CONT_TOK // ctx_size
    rows = tokens.shape[0]
    n_halo = 1 + -(-(LONGEST - 1) // cont_dev)
    lengths = cont_lengths[0]

    cont_at = me * cont_dev + jnp.arange(cont_dev, dtype=jnp.int32)
    cont_ends = jnp.cumsum(lengths)
    starts = cont_ends - lengths
    seg = jnp.sum((cont_ends[None, :] <= cont_at[:, None]).astype(jnp.int32), axis=1)
    slots = jnp.arange(lengths.shape[0], dtype=jnp.int32)
    first = jnp.sum(jnp.where(slots[None, :] == seg[:, None], starts[None, :], 0), axis=1)
    position = jnp.concatenate(
        [me * prompt_dev + jnp.arange(prompt_dev, dtype=jnp.int32), PROMPT + cont_at - first]
    )
    low = first - me * cont_dev
    low_col = jnp.broadcast_to(low[:, None], (cont_dev, 128))
    low_row = jnp.broadcast_to(jnp.concatenate([low, low])[None, :], (8, 2 * cont_dev))
    lo_first = low[0]
    tables = rotary_tables(position)

    gains = jnp.concatenate([attn_gain, ffn_gain, query_gain, key_gain])[None]
    spread = jnp.where(jnp.arange(parts)[:, None] == part, gains, jnp.zeros((), BF))
    gains = butterfly(spread, ("ctx", "shard"))
    wide, narrow = attn_gain.shape[0], query_gain.shape[0]
    full_attn_gain = gains[:, :wide].reshape(-1).astype(F32)
    full_ffn_gain = gains[:, wide : 2 * wide].reshape(-1).astype(F32)
    full_query_gain = gains[:, 2 * wide : 2 * wide + narrow].reshape(-1).astype(F32)
    full_key_gain = gains[:, 2 * wide + narrow :].reshape(-1).astype(F32)
    q_cols, k_cols = w_query.shape[1], key_weight.shape[1]
    w_qkv = lax.all_gather(
        jnp.concatenate([w_query, key_weight, value_weight], axis=1), weight_axes, axis=0, tiled=True
    )
    o_cols, f_cols = w_out.shape[0], w_gate.shape[1]
    w_rest = lax.all_gather(
        jnp.concatenate([w_out.T, w_gate, w_up, w_down.T], axis=1), weight_axes, axis=0, tiled=True
    )
    full_q, full_k, full_v = (
        w_qkv[:, :q_cols],
        w_qkv[:, q_cols : q_cols + k_cols],
        w_qkv[:, q_cols + k_cols :],
    )
    out_t, full_gate, full_up, down_t = (
        w_rest[:, :o_cols],
        w_rest[:, o_cols : o_cols + f_cols],
        w_rest[:, o_cols + f_cols : o_cols + 2 * f_cols],
        w_rest[:, o_cols + 2 * f_cols :],
    )

    fold = LOG2E / math.sqrt(HEAD_SIZE)

    def query_chain(linear, gain_vec):
        return rotary(root_mean_gain(linear.reshape(rows, -1, HEAD_SIZE), gain_vec), tables)

    inputs = tokens.astype(F32)
    normed_f, norm_one_back = jax.vjp(root_mean_gain, inputs, full_attn_gain)
    normed = normed_f.astype(BF)
    k_linear = mm(normed, full_k)
    v_linear = mm(normed, full_v)
    q_linear = mm(normed, full_q)
    key_f, key_back = jax.vjp(query_chain, k_linear, full_key_gain)
    query_f, query_back = jax.vjp(query_chain, q_linear, full_query_gain)
    keys = key_f.astype(BF).reshape(rows, -1)
    values = v_linear.astype(BF)
    queries = (query_f * fold).astype(BF).reshape(rows, -1)
    k_slots, v_slots = gather_slots(keys[:prompt_dev], values[:prompt_dev])
    k_own, v_own = keys[prompt_dev:], values[prompt_dev:]
    if n_halo == 3:
        odd = (me % 2) == 1
        k2, v2 = shift(k_own, 2), shift(v_own, 2)
        k1 = swap(jnp.where(odd, k2, k_own), "ctx", 1)
        v1 = swap(jnp.where(odd, v2, v_own), "ctx", 1)
        k_halo, v_halo = [k_own, k1, k2], [v_own, v1, v2]
    else:
        k_halo = [k_own] + [shift(k_own, d) for d in range(1, n_halo)]
        v_halo = [v_own] + [shift(v_own, d) for d in range(1, n_halo)]
    attended, lse = attention_forward(
        me, lo_first, queries, low_col, k_slots, v_slots, k_halo, v_halo, prompt_dev, cont_dev
    )
    attended_low = attended.astype(BF)
    residual = inputs + exchange(mm(attended_low, out_t, NT))
    normed_ffn_f, norm_two_back = jax.vjp(root_mean_gain, residual, full_ffn_gain)
    normed_ffn = normed_ffn_f.astype(BF)
    gate_proj = mm(normed_ffn, full_gate)
    up_proj = mm(normed_ffn, full_up)
    hidden_f, swiglu_back = jax.vjp(swiglu, gate_proj, up_proj)
    hidden = hidden_f.astype(BF)
    layer_out = (residual + exchange(mm(hidden, down_t, NT))).astype(BF)

    grad_hidden = mm(cotangent, down_t)
    grad_gate_f, grad_up_f = swiglu_back(grad_hidden)
    grad_gate, grad_upper = grad_gate_f.astype(BF), grad_up_f.astype(BF)
    grad_normed_ffn = exchange(mm(grad_gate, full_gate, NT) + mm(grad_upper, full_up, NT))
    grad_resid_norm, grad_ffn_gain_local = norm_two_back(grad_normed_ffn)
    grad_resid = cotangent.astype(F32) + grad_resid_norm
    grad_mixed = grad_resid.astype(BF)
    grad_attended = mm(grad_mixed, out_t).astype(BF)
    rest_grads = jnp.concatenate(
        [
            mm(grad_mixed, attended_low, TN).astype(BF),
            mm(normed_ffn, grad_gate, TN).astype(BF),
            mm(normed_ffn, grad_upper, TN).astype(BF),
            mm(cotangent, hidden, TN).astype(BF),
        ],
        axis=1,
    )
    rest_share = lax.psum_scatter(rest_grads, weight_axes, scatter_dimension=0, tiled=True)

    grad_query, dk_slots, dv_slots, dk_halo, dv_halo = attention_backward(
        me, lo_first, queries, grad_attended, attended, lse, low_row,
        k_slots, v_slots, k_halo, v_halo, prompt_dev, cont_dev,
    )
    dk_prompt, dv_prompt = scatter_slots(dk_slots, dv_slots)
    if n_halo == 3:
        k1, v1 = swap(dk_halo[1], "ctx", 1), swap(dv_halo[1], "ctx", 1)
        zero = jnp.zeros((), BF)
        k2 = shift(add_low(dk_halo[2], jnp.where(odd, k1, zero)), -2)
        v2 = shift(add_low(dv_halo[2], jnp.where(odd, v1, zero)), -2)
        dk_cont = dk_halo[0].astype(F32) + jnp.where(odd, zero, k1).astype(F32) + k2.astype(F32)
        dv_cont = dv_halo[0].astype(F32) + jnp.where(odd, zero, v1).astype(F32) + v2.astype(F32)
    else:
        dk_cont, dv_cont = dk_halo[0].astype(F32), dv_halo[0].astype(F32)
        for d in range(1, n_halo):
            dk_cont = dk_cont + shift(dk_halo[d], -d).astype(F32)
            dv_cont = dv_cont + shift(dv_halo[d], -d).astype(F32)
    grad_key = jnp.concatenate([dk_prompt.astype(F32), dk_cont])
    grad_value = jnp.concatenate([dv_prompt.astype(F32), dv_cont])
    grad_q_linear, grad_query_gain_part = query_back(grad_query.reshape(rows, -1, HEAD_SIZE))
    grad_k_linear, grad_key_gain_part = key_back(grad_key.reshape(rows, -1, HEAD_SIZE))
    grad_qkv = jnp.concatenate(
        [grad_q_linear.astype(BF), grad_k_linear.astype(BF), grad_value.astype(BF)], axis=1
    )
    grad_normed = exchange(mm(grad_qkv, w_qkv, NT))
    qkv_share = lax.psum_scatter(
        mm(normed, grad_qkv, TN).astype(BF), weight_axes, scatter_dimension=0, tiled=True
    )
    grad_inputs_norm, grad_attn_gain_local = norm_one_back(grad_normed)
    grad_tokens = (grad_resid + grad_inputs_norm).astype(BF)
    model_gains = jnp.concatenate([grad_attn_gain_local, grad_ffn_gain_local])
    model_gains = butterfly(model_gains, ("ctx", "shard")).reshape(2, parts, wide)
    head_gains = jnp.concatenate([grad_query_gain_part, grad_key_gain_part])
    head_gains = butterfly(head_gains, ("ctx", "shard", "tensor")).reshape(2, parts, narrow)
    model_gains = lax.dynamic_index_in_dim(model_gains, part, 1, keepdims=False)
    head_gains = lax.dynamic_index_in_dim(head_gains, part, 1, keepdims=False)
    qkv_share = qkv_share.astype(F32)
    rest_share = rest_share.astype(F32)
    return (
        layer_out,
        grad_tokens,
        model_gains[0],
        model_gains[1],
        head_gains[0],
        head_gains[1],
        qkv_share[:, :q_cols],
        qkv_share[:, q_cols : q_cols + k_cols],
        qkv_share[:, q_cols + k_cols :],
        rest_share[:, :o_cols].T,
        rest_share[:, o_cols : o_cols + f_cols],
        rest_share[:, o_cols + f_cols : o_cols + 2 * f_cols],
        rest_share[:, o_cols + 2 * f_cols :].T,
    )


def solution(mesh):
    split = ("shard", "ctx")
    rows, gain = P(split, None), P(split)
    into, out_of = P(split, "tensor"), P("tensor", split)
    in_specs = (rows, P("shard", None)) + (gain,) * 4 + (into,) * 3 + (out_of,)
    in_specs += (into, into, out_of, rows)
    out_specs = (rows, rows) + (gain,) * 4 + (into,) * 3 + (out_of, into, into, out_of)
    return jax.shard_map(body, mesh=mesh, in_specs=in_specs, out_specs=out_specs, check_vma=False)
```

time: 2350 us -> 897 us (0.38)
  matrix products: 906 us -> 96.8 us
  waiting for transfers between devices: 1010 us -> 371 us
  starting transfers between devices: 1.05 us -> 157 us
  blocking collectives: 110 us -> 0 us
  Pallas kernels: 0 us -> 96.2 us
  other arithmetic: 152 us -> 85.3 us
  local copies, waits for them, and re-layouts: 132 us -> 69.5 us
    dot_general x63 -> x17, matrix products: 906 us -> 96.8 us  [mm(): return lax.dot_general(left, right, dims, preferred_element_type=F32)]
    reduce_scatter x9 -> x2, waiting for transfers between devices: 615 us -> 52.9 us  [the longest x1 52.9 us: body(): lax.psum_scatter(rest_grads, weight_axes, scatter_dimension=0, tiled=True)]
    ppermute x0 -> x53, waiting for transfers between devices: none -> 287 us  [the longest x49 237 us: swap(): return lax.ppermute(value, axis, [(i, i ^ bit) for i in range(size)])]
    all_gather x9 -> x2, waiting for transfers between devices: 217 us -> 31.2 us  [the longest x1 31.2 us: body(): lax.all_gather(jnp.concatenate([w_query, key_weight, value_weight], axis=...]
    psum x3 -> x0, waiting for transfers between devices: 177 us -> none  [the longest x1 62.5 us: body(): lax.psum(ffn_back_part.astype(jnp.bfloat16), 'tensor').astype(jnp.float32)]
    ppermute x0 -> x53, starting transfers between devices: none -> 156 us  [the longest x49 147 us: swap(): return lax.ppermute(value, axis, [(i, i ^ bit) for i in range(size)])]
    unnamed x2 -> x0, blocking collectives: 105 us -> none
    pallas_call x0 -> x2, Pallas kernels: none -> 96.2 us  [the longest x1 67.3 us: attention_backward(): pl.pallas_call(functools.partial(bwd_kernel, n_slots, n_halo, prompt, con...]
  transfers between devices with their start and end apart: 21 -> 57, of which waited for: 18 -> 23; matrix products, arithmetic and copies ran while one was open for 18% -> 18% of each run, Pallas kernels for 0% -> 3%
where the time goes in v1:
time: 897 us; the launch traced here: 891 us
  waiting for transfers between devices  371 us (41%)
  starting transfers between devices  157 us (18%)
  matrix products  96.8 us (11%)
  Pallas kernels  96.2 us (11%)
  other arithmetic  85.3 us (10%)
  local copies, waits for them, and re-layouts  69.5 us (8%)
  between operations  15.5 us (2%)
    ppermute x49, waiting for transfers between devices, swap(): return lax.ppermute(value, axis, [(i, i ^ bit) for i in range(size)])  237 us
    ppermute x49, starting transfers between devices, swap(): return lax.ppermute(value, axis, [(i, i ^ bit) for i in range(size)])  147 us
    dot_general x17, matrix products, mm(): return lax.dot_general(left, right, dims, preferred_element_type=F32)  96.8 us
    pallas_call x1, Pallas kernels, attention_backward(): pl.pallas_call(functools.partial(bwd_kernel, n_slots, n_halo, prompt, con...  67.3 us
    reduce_scatter x1, waiting for transfers between devices, body(): lax.psum_scatter(rest_grads, weight_axes, scatter_dimension=0, tiled=True)  52.9 us
    ppermute x4, waiting for transfers between devices, shift(): lax.ppermute(value, 'ctx', [(i, i + by) for i in range(size) if 0 <= i +...  49.7 us
    all_gather x1, waiting for transfers between devices, body(): lax.all_gather(jnp.concatenate([w_query, key_weight, value_weight], axis=...  31.2 us
    pallas_call x1, Pallas kernels, attention_forward(): pl.pallas_call(functools.partial(fwd_kernel, n_slots, n_halo, prompt, con...  28.9 us
  transfers between devices with their start and end apart: 57, of which 23 were waited for; matrix products, arithmetic and copies ran while one was open for 18% of the time, Pallas kernels for 3%

profile of v1, /device:TPU:0, one launch (start us, length us, event | category | flops | bytes accessed | tf_op | source)
XLA Modules:
  0.0 890.8 jit_solution(8105612171573524121)
XLA Ops:
  31.7 5.4 copy.114
  37.5 31.2 %all-gather.3.cloned.1.call-done = bf16[1024,2048]{1,0:T(8,128)(2,1)} async-done(((bf16[64,2048]{1,0:T(8,128)(2,1)}), bf16[1024,2048]{1,0:T(8,128)(2,1)}) %all-gather.3.cloned.1.call-update) | async-done | bytes 4194320 | tf_op jit(solution)/shard_map/all_gather | solution.py:416
  89.3 24.5 %collective-permute-done.18.refs_18_ = bf16[512,512]{1,0:T(8,128)(2,1)S(1)} collective-permute-done((bf16[512,512]{1,0:T(8,128)(2,1)S(1)}, bf16[512,512]{1,0:T(8,128)(2,1)S(1)}, u32[]{:S(2)}, u32[]{:S(2)}) %collective-permute-start.18) | collective-permute-done | bytes 524320 | tf_op jit(solution)/shard_map/ppermute | solution.py:318
  113.9 12.1 %collective-permute-done.20.refs_21_ = bf16[512,512]{1,0:T(8,128)(2,1)S(1)} collective-permute-done((bf16[512,512]{1,0:T(8,128)(2,1)S(1)}, bf16[512,512]{1,0:T(8,128)(2,1)S(1)}, u32[]{:S(2)}, u32[]{:S(2)}) %collective-permute-start.20) | collective-permute-done | bytes 524320 | tf_op jit(solution)/shard_map/ppermute | solution.py:318
  133.4 37.8 %collective-permute-done.9.refs_6_ = bf16[512,512]{1,0:T(8,128)(2,1)S(1)} collective-permute-done((bf16[512,512]{1,0:T(8,128)(2,1)S(1)}, bf16[512,512]{1,0:T(8,128)(2,1)S(1)}, u32[]{:S(2)}, u32[]{:S(2)}) %collective-permute-start.9) | collective-permute-done | bytes 524320 | tf_op jit(solution)/shard_map/ppermute | solution.py:269
  175.9 5.4 copy.87
  181.2 5.2 maximum_multiply_fusion
  186.5 5.3 copy.115
  194.3 5.4 copy.113
  200.8 9.3 %multiply_convert_fusion.2.q_ref = bf16[1024,1024]{1,0:T(8,128)(2,1)} fusion(f32[1024,1024]{1,0:T(8,128)} %copy.115, f32[1024,1024]{1,0:T(8,128)} %copy.114, f32[1024,1024]{1,0:T(8,128)} %copy.87, f32[1024,1024]{1,0:T(8,128)} %copy.113, f32[1024]{0:T(1024)S(1)} %broadcast_bitcast_fusion), kind=kLoop, calls=%fused_computation.42 | loop fusion | flops 6291456 | bytes 18878464 | tf_op jit(solution)/shard_map/convert_element_type | solution.py:450
  211.5 28.9 %attention_forward.1 = (f32[1024,1024]{1,0:T(8,128)}, f32[4,8,1024]{2,1,0:T(8,128)S(1)}) custom-call(s32[2]{0:T(128)S(1)} %pad_add_fusion.3.idx_ref, bf16[1024,1024]{1,0:T(8,128)(2,1)} %multiply_convert_fusion.2.q_ref, s32[512,128]{1,0:T(8,128)S(1)} %broadcast_in_dim.91.lo_ref, bf16[512,512]{1,0:T(8,128)(2,1)S(1)} %copy.116.refs_0_, ...), custom_call_target="tpu_custom_call" | custom-call | flops 20401094656 | bytes 25165824 | tf_op jit(solution)/shard_map/attention_forward/pallas_call | solution.py:105
  241.2 6.6 convolution_convert_fusion.7
  247.9 6.1 fusion.18
  254.0 37.2 %collective-permute-done.22 = bf16[1024,1024]{0,1:T(8,128)(2,1)} collective-permute-done((bf16[1024,1024]{0,1:T(8,128)(2,1)}, bf16[1024,1024]{0,1:T(8,128)(2,1)}, u32[]{:S(2)}, u32[]{:S(2)}) %collective-permute-start.22) | collective-permute-done | bytes 2097184 | tf_op jit(solution)/shard_map/ppermute | solution.py:269
  297.3 5.6 fusion.24
  302.9 11.0 %fusion.2 = (bf16[1024,1536]{1,0:T(8,128)(2,1)}, bf16[1024,1536]{1,0:T(8,128)(2,1)}, bf16[1024,1536]{1,0:T(8,128)(2,1)}) fusion(f32[1024,1536]{1,0:T(8,128)} %fusion.24, f32[1536,1024]{0,1:T(8,128)S(1)} %fusion.18, bf16[1024,1024]{0,1:T(8,128)(2,1)S(1)} %multiply_convert_fusion.1, bf16[1024,5632]{1,0:T(8,128)(2,1)S(1)} %bitcast.87), kind=kOutput, calls=%fused_computation.9 | convolution fusion | flops 3246391296 | bytes 27262976 | tf_op jit(solution)/shard_map/dot_general | solution.py:30
  313.9 5.5 fusion.22
  319.4 4.7 add_convert_fusion
  324.1 4.6 fusion.35
  333.6 35.0 %collective-permute-done.24 = bf16[1024,1024]{0,1:T(8,128)(2,1)} collective-permute-done((bf16[1024,1024]{0,1:T(8,128)(2,1)}, bf16[1024,1024]{0,1:T(8,128)(2,1)}, u32[]{:S(2)}, u32[]{:S(2)}) %collective-permute-start.24) | collective-permute-done | bytes 2097184 | tf_op jit(solution)/shard_map/ppermute | solution.py:269
  368.6 5.5 multiply_reduce_fusion.1
  374.1 39.5 %collective-permute-done.23 = bf16[1024,1024]{0,1:T(8,128)(2,1)} collective-permute-done((bf16[1024,1024]{0,1:T(8,128)(2,1)}, bf16[1024,1024]{0,1:T(8,128)(2,1)}, u32[]{:S(2)}, u32[]{:S(2)}) %collective-permute-start.23) | collective-permute-done | bytes 2097184 | tf_op jit(solution)/shard_map/ppermute | solution.py:269
  413.5 6.5 fusion.9
  420.0 6.9 convolution_convert_fusion.6.do_ref
  426.9 67.3 %attention_backward.1 = (f32[1024,1024]{1,0:T(8,128)}, bf16[512,512]{1,0:T(8,128)(2,1)S(1)}, bf16[512,512]{1,0:T(8,128)(2,1)S(1)}, bf16[512,512]{1,0:T(8,128)(2,...) custom-call(s32[2]{0:T(128)S(1)} %pad_add_fusion.3.idx_ref, ...), custom_call_target="tpu_custom_call" | custom-call | flops 51002736640 | bytes 41943040 | tf_op jit(solution)/shard_map/attention_backward/pallas_call | solution.py:228
  494.2 5.4 copy.118
  503.4 16.2 %collective-permute-start.26 = (bf16[512,512]{1,0:T(8,128)(2,1)S(1)}, bf16[512,512]{1,0:T(8,128)(2,1)S(1)}, u32[]{:S(2)}, u32[]{:S(2)}) collective-permute-start(bf16[512,512]{1,0:T(8,128)(2,1)S(1)} %copy-done.81), channel_id=1, source_target_pairs={{0,2},{2,0},{4,6},{6,4},{8,10},{10,8},{12,14},{14,12},{1,3},{3,1},... | collective-permute-start | bytes 1572872 | tf_op jit(solution)/shard_map/ppermute | solution.py:269
  532.9 28.1 %collective-permute-start.30 = (bf16[512,512]{1,0:T(8,128)(2,1)S(1)}, bf16[512,512]{1,0:T(8,128)(2,1)S(1)}, u32[]{:S(2)}, u32[]{:S(2)}) collective-permute-start(bf16[512,512]{1,0:T(8,128)(2,1)S(1)} %add_convert_fusion.12), channel_id=1, source_target_pairs={{0,4},{2,6},{4,0},{6,2},{8,12},{10,14},{12,8},{14,10},{1,5},{3,7},... | collective-permute-start | bytes 1572872 | tf_op jit(solution)/shard_map/ppermute | solution.py:269
  561.9 11.5 %collective-permute-done.42 = bf16[512,512]{1,0:T(8,128)(2,1)S(1)} collective-permute-done((bf16[512,512]{1,0:T(8,128)(2,1)S(1)}, bf16[512,512]{1,0:T(8,128)(2,1)S(1)}, u32[]{:S(2)}, u32[]{:S(2)}) %collective-permute-start.42) | collective-permute-done | bytes 524320 | tf_op jit(solution)/shard_map/ppermute | solution.py:318
  573.4 35.2 %collective-permute-start.37 = (bf16[512,512]{1,0:T(8,128)(2,1)S(1)}, bf16[512,512]{1,0:T(8,128)(2,1)S(1)}, u32[]{:S(2)}, u32[]{:S(2)}) collective-permute-start(bf16[512,512]{1,0:T(8,128)(2,1)S(1)} %add_convert_fusion.7), channel_id=1, source_target_pairs={{0,8},{2,10},{4,12},{6,14},{8,0},{10,2},{12,4},{14,6},{1,9},{3,11}... | collective-permute-start | bytes 1572872 | tf_op jit(solution)/shard_map/ppermute | solution.py:269
  613.9 5.9 collective-permute-done.37
  619.8 3.8 collective-permute-start.31
  626.3 9.8 %collective-permute-start.40 = (bf16[512,512]{1,0:T(8,128)(2,1)}, bf16[512,512]{1,0:T(8,128)(2,1)}, u32[]{:S(2)}, u32[]{:S(2)}) collective-permute-start(bf16[512,512]{1,0:T(8,128)(2,1)} %add_convert_fusion.5), channel_id=1, source_target_pairs={{0,8},{2,10},{4,12},{6,14},{8,0},{10,2},{12,4},{14,6},{1,9},{3,11}... | collective-permute-start | bytes 1572872 | tf_op jit(solution)/shard_map/ppermute | solution.py:269
  655.5 8.3 convolution_convert_fusion.3
  663.9 7.7 convolution_convert_fusion.1
  671.7 5.1 convolution_convert_fusion.2
  676.8 4.9 fusion.17
  681.7 3.8 convolution_convert_fusion.5
  685.5 4.0 copy.104
  689.4 10.0 %pad_maximum_fusion = bf16[1024,5632]{1,0:T(8,128)(2,1)} fusion(bf16[1024,1536]{1,0:T(8,128)(2,1)} %fusion.17, bf16[1024,1536]{1,0:T(8,128)(2,1)} %convolution_convert_fusion.1, bf16[1024,1536]{1,0:T(8,128)(2,1)} %convolution_convert_fusion.2, bf16[1024,1024]{1,0:T(8,128)(2,1)} %copy.104), kind=kLoop, calls=%fused_computation | loop fusion | flops 46137344 | bytes 23068672 | tf_op jit(solution)/shard_map/concatenate | solution.py:483
  699.5 7.7 convolution_convert_fusion.4
  707.4 62.3 %collective-permute-done.43 = bf16[1024,1024]{0,1:T(8,128)(2,1)S(1)} collective-permute-done((bf16[1024,1024]{0,1:T(8,128)(2,1)S(1)}, bf16[1024,1024]{0,1:T(8,128)(2,1)S(1)}, u32[]{:S(2)}, u32[]{:S(2)}) %collective-permute-start.43) | collective-permute-done | bytes 2097184 | tf_op jit(solution)/shard_map/ppermute | solution.py:269
  775.4 14.2 %collective-permute-start.50 = (f32[256]{0:T(256)S(1)}, f32[256]{0:T(256)S(1)}, u32[]{:S(2)}, u32[]{:S(2)}) collective-permute-start(f32[256]{0:T(256)S(1)} %add.286), channel_id=1, source_target_pairs={{0,8},{2,10},{4,12},{6,14},{8,0},{10,2},{12,4},{14,6},{1,9},{3,11}... | collective-permute-start | bytes 3080 | tf_op jit(solution)/shard_map/ppermute | solution.py:269
  795.8 4.2 copy.105
  808.7 4.2 collective-permute-start.47
  812.9 6.4 fusion.12
  819.3 3.9 copy.106
  827.1 52.9 %reduce-scatter.5.cloned.1.call-done = bf16[64,5632]{1,0:T(8,128)(2,1)} async-done(((bf16[1024,5632]{1,0:T(8,128)(2,1)}), bf16[64,5632]{1,0:T(8,128)(2,1)}) %reduce-scatter.5.cloned.1.call-update) | async-done | bytes 720912 | tf_op jit(solution)/shard_map/reduce_scatter | solution.py:492
  (389 shorter events, 147.4 us)
Async XLA Ops:
  7.2 61.5 %all-gather.3.cloned.1.call-start = ((), (), s32[]{:S(2)}) async-start(), calls=%async_computation.2 | async-start | bytes 4456448 | tf_op jit(solution)/shard_map/all_gather | solution.py:416
  9.0 232.3 %all-gather.5.cloned.1.call-start = ((), (), s32[]{:S(2)}) async-start(), calls=%async_computation.3 | async-start | bytes 12255232 | tf_op jit(solution)/shard_map/all_gather | solution.py:420
  11.2 812.7 %reduce-scatter.3.cloned.1.call-start = ((), (), s32[]{:S(2)}) async-start(), calls=%async_computation.4 | async-start | bytes 4456448 | tf_op jit(solution)/shard_map/reduce_scatter | solution.py:519
  12.1 5.2 collective-permute-start
  25.3 11.7 %collective-permute-start.3 = (bf16[16,144]{1,0:T(8,128)(2,1)S(1)}, bf16[16,144]{1,0:T(8,128)(2,1)S(1)}, u32[]{:S(2)}, u32[]{:S(2)}) collective-permute-start(bf16[16,144]{1,0:T(8,128)(2,1)S(1)} %add.238), channel_id=1, source_target_pairs={{0,16},{16,0},{1,17},{17,1},{2,18},{18,2},{3,19},{19,3},{4,20},{20... | collective-permute-start | bytes 13832 | tf_op jit(solution)/shard_map/ppermute | solution.py:269
  73.8 55.8 %collective-permute-start.7 = (bf16[512,512]{1,0:T(8,128)(2,1)S(1)}, bf16[512,512]{1,0:T(8,128)(2,1)S(1)}, u32[]{:S(2)}, u32[]{:S(2)}) collective-permute-start(bf16[512,512]{1,0:T(8,128)(2,1)S(1)} %copy.116.refs_0_), channel_id=1, source_target_pairs={{0,8},{2,10},{4,12},{6,14},{8,0},{10,2},{12,4},{14,6},{1,9},{3,11}... | collective-permute-start | bytes 1572872 | tf_op jit(solution)/shard_map/ppermute | solution.py:269
  75.3 55.5 %collective-permute-start.5 = (bf16[512,512]{1,0:T(8,128)(2,1)S(1)}, bf16[512,512]{1,0:T(8,128)(2,1)S(1)}, u32[]{:S(2)}, u32[]{:S(2)}) collective-permute-start(bf16[512,512]{1,0:T(8,128)(2,1)S(1)} %copy.116.refs_0_), channel_id=1, source_target_pairs={{0,4},{2,6},{4,0},{6,2},{8,12},{10,14},{12,8},{14,10},{1,5},{3,7},... | collective-permute-start | bytes 1572872 | tf_op jit(solution)/shard_map/ppermute | solution.py:269
  76.8 56.0 %collective-permute-start.4 = (bf16[512,512]{1,0:T(8,128)(2,1)S(1)}, bf16[512,512]{1,0:T(8,128)(2,1)S(1)}, u32[]{:S(2)}, u32[]{:S(2)}) collective-permute-start(bf16[512,512]{1,0:T(8,128)(2,1)S(1)} %copy.116.refs_0_), channel_id=1, source_target_pairs={{0,2},{2,0},{4,6},{6,4},{8,10},{10,8},{12,14},{14,12},{1,3},{3,1},... | collective-permute-start | bytes 1572872 | tf_op jit(solution)/shard_map/ppermute | solution.py:269
  77.1 36.7 %collective-permute-start.18 = (bf16[512,512]{1,0:T(8,128)(2,1)S(1)}, bf16[512,512]{1,0:T(8,128)(2,1)S(1)}, u32[]{:S(2)}, u32[]{:S(2)}) collective-permute-start(bf16[512,512]{1,0:T(8,128)(2,1)S(1)} %copy.117.refs_16_), channel_id=1, source_target_pairs={{0,4},{2,6},{4,8},{6,10},{8,12},{10,14},{1,5},{3,7},{5,9},{7,11},{... | collective-permute-start | bytes 1572872 | tf_op jit(solution)/shard_map/ppermute | solution.py:318
  83.3 42.8 %collective-permute-start.20 = (bf16[512,512]{1,0:T(8,128)(2,1)S(1)}, bf16[512,512]{1,0:T(8,128)(2,1)S(1)}, u32[]{:S(2)}, u32[]{:S(2)}) collective-permute-start(bf16[512,512]{1,0:T(8,128)(2,1)S(1)} %slice.149.refs_19_), channel_id=1, source_target_pairs={{0,4},{2,6},{4,8},{6,10},{8,12},{10,14},{1,5},{3,7},{5,9},{7,11},{... | collective-permute-start | bytes 1572872 | tf_op jit(solution)/shard_map/ppermute | solution.py:318
  113.9 19.0 %collective-permute-start.19 = (bf16[512,512]{1,0:T(8,128)(2,1)S(1)}, bf16[512,512]{1,0:T(8,128)(2,1)S(1)}, u32[]{:S(2)}, u32[]{:S(2)}) collective-permute-start(bf16[512,512]{1,0:T(8,128)(2,1)S(1)} %broadcast_select_fusion.1), channel_id=1, source_target_pairs={{0,2},{2,0},{4,6},{6,4},{8,10},{10,8},{12,14},{14,12},{1,3},{3,1},... | collective-permute-start | bytes 1572872 | tf_op jit(solution)/shard_map/ppermute | solution.py:269
  127.1 44.1 %collective-permute-start.12 = (bf16[512,512]{1,0:T(8,128)(2,1)S(1)}, bf16[512,512]{1,0:T(8,128)(2,1)S(1)}, u32[]{:S(2)}, u32[]{:S(2)}) collective-permute-start(bf16[512,512]{1,0:T(8,128)(2,1)S(1)} %get-tuple-element.141.refs_8_), channel_id=1, source_target_pairs={{0,4},{2,6},{4,0},{6,2},{8,12},{10,14},{12,8},{14,10},{1,5},{3,7},... | collective-permute-start | bytes 1572872 | tf_op jit(solution)/shard_map/ppermute | solution.py:269
  129.6 41.6 %collective-permute-start.9 = (bf16[512,512]{1,0:T(8,128)(2,1)S(1)}, bf16[512,512]{1,0:T(8,128)(2,1)S(1)}, u32[]{:S(2)}, u32[]{:S(2)}) collective-permute-start(bf16[512,512]{1,0:T(8,128)(2,1)S(1)} %collective-permute-done.7.refs_4_), channel_id=1, source_target_pairs={{0,4},{2,6},{4,0},{6,2},{8,12},{10,14},{12,8},{14,10},{1,5},{3,7},... | collective-permute-start | bytes 1572872 | tf_op jit(solution)/shard_map/ppermute | solution.py:269
  130.8 69.4 %collective-permute-start.14 = (bf16[512,512]{1,0:T(8,128)(2,1)S(1)}, bf16[512,512]{1,0:T(8,128)(2,1)}, u32[]{:S(2)}, u32[]{:S(2)}) collective-permute-start(bf16[512,512]{1,0:T(8,128)(2,1)S(1)} %get-tuple-element.141.refs_8_), channel_id=1, source_target_pairs={{0,8},{2,10},{4,12},{6,14},{8,0},{10,2},{12,4},{14,6},{1,9},{3,11}... | collective-permute-start | bytes 1572872 | tf_op jit(solution)/shard_map/ppermute | solution.py:269
  132.9 67.4 %collective-permute-start.11 = (bf16[512,512]{1,0:T(8,128)(2,1)S(1)}, bf16[512,512]{1,0:T(8,128)(2,1)}, u32[]{:S(2)}, u32[]{:S(2)}) collective-permute-start(bf16[512,512]{1,0:T(8,128)(2,1)S(1)} %get-tuple-element.141.refs_8_), channel_id=1, source_target_pairs={{0,2},{2,0},{4,6},{6,4},{8,10},{10,8},{12,14},{14,12},{1,3},{3,1},... | collective-permute-start | bytes 1572872 | tf_op jit(solution)/shard_map/ppermute | solution.py:269
  132.9 66.8 %collective-permute-start.8 = (bf16[512,512]{1,0:T(8,128)(2,1)S(1)}, bf16[512,512]{1,0:T(8,128)(2,1)}, u32[]{:S(2)}, u32[]{:S(2)}) collective-permute-start(bf16[512,512]{1,0:T(8,128)(2,1)S(1)} %collective-permute-done.7.refs_4_), channel_id=1, source_target_pairs={{0,2},{2,0},{4,6},{6,4},{8,10},{10,8},{12,14},{14,12},{1,3},{3,1},... | collective-permute-start | bytes 1572872 | tf_op jit(solution)/shard_map/ppermute | solution.py:269
  171.2 28.5 %collective-permute-start.6 = (bf16[512,512]{1,0:T(8,128)(2,1)S(1)}, bf16[512,512]{1,0:T(8,128)(2,1)}, u32[]{:S(2)}, u32[]{:S(2)}) collective-permute-start(bf16[512,512]{1,0:T(8,128)(2,1)S(1)} %collective-permute-done.5.refs_2_), channel_id=1, source_target_pairs={{0,2},{2,0},{4,6},{6,4},{8,10},{10,8},{12,14},{14,12},{1,3},{3,1},... | collective-permute-start | bytes 1572872 | tf_op jit(solution)/shard_map/ppermute | solution.py:269
  172.0 28.8 %collective-permute-start.16 = (bf16[512,512]{1,0:T(8,128)(2,1)S(1)}, bf16[512,512]{1,0:T(8,128)(2,1)}, u32[]{:S(2)}, u32[]{:S(2)}) collective-permute-start(bf16[512,512]{1,0:T(8,128)(2,1)S(1)} %collective-permute-done.12.refs_10_), channel_id=1, source_target_pairs={{0,8},{2,10},{4,12},{6,14},{8,0},{10,2},{12,4},{14,6},{1,9},{3,11}... | collective-permute-start | bytes 1572872 | tf_op jit(solution)/shard_map/ppermute | solution.py:269
  199.7 10.5 %collective-permute-start.21 = (bf16[512,512]{1,0:T(8,128)(2,1)}, bf16[512,512]{1,0:T(8,128)(2,1)S(1)}, u32[]{:S(2)}, u32[]{:S(2)}) collective-permute-start(bf16[512,512]{1,0:T(8,128)(2,1)} %get-tuple-element.140), channel_id=1, source_target_pairs={{0,2},{2,0},{4,6},{6,4},{8,10},{10,8},{12,14},{14,12},{1,3},{3,1},... | collective-permute-start | bytes 1572872 | tf_op jit(solution)/shard_map/ppermute | solution.py:269
  199.7 10.5 %collective-permute-start.13 = (bf16[512,512]{1,0:T(8,128)(2,1)S(1)}, bf16[512,512]{1,0:T(8,128)(2,1)S(1)}, u32[]{:S(2)}, u32[]{:S(2)}) collective-permute-start(bf16[512,512]{1,0:T(8,128)(2,1)S(1)} %collective-permute-done.12.refs_10_), channel_id=1, source_target_pairs={{0,2},{2,0},{4,6},{6,4},{8,10},{10,8},{12,14},{14,12},{1,3},{3,1},... | collective-permute-start | bytes 1572872 | tf_op jit(solution)/shard_map/ppermute | solution.py:269
  200.2 10.0 %collective-permute-start.10 = (bf16[512,512]{1,0:T(8,128)(2,1)}, bf16[512,512]{1,0:T(8,128)(2,1)S(1)}, u32[]{:S(2)}, u32[]{:S(2)}) collective-permute-start(bf16[512,512]{1,0:T(8,128)(2,1)} %copy-done.6), channel_id=1, source_target_pairs={{0,2},{2,0},{4,6},{6,4},{8,10},{10,8},{12,14},{14,12},{1,3},{3,1},... | collective-permute-start | bytes 1572872 | tf_op jit(solution)/shard_map/ppermute | solution.py:269
  200.3 9.9 %collective-permute-start.15 = (bf16[512,512]{1,0:T(8,128)(2,1)}, bf16[512,512]{1,0:T(8,128)(2,1)S(1)}, u32[]{:S(2)}, u32[]{:S(2)}) collective-permute-start(bf16[512,512]{1,0:T(8,128)(2,1)} %collective-permute-done.14.refs_12_), channel_id=1, source_target_pairs={{0,2},{2,0},{4,6},{6,4},{8,10},{10,8},{12,14},{14,12},{1,3},{3,1},... | collective-permute-start | bytes 1572872 | tf_op jit(solution)/shard_map/ppermute | solution.py:269
  200.7 9.5 %collective-permute-start.17 = (bf16[512,512]{1,0:T(8,128)(2,1)}, bf16[512,512]{1,0:T(8,128)(2,1)S(1)}, u32[]{:S(2)}, u32[]{:S(2)}) collective-permute-start(bf16[512,512]{1,0:T(8,128)(2,1)} %collective-permute-done.16.refs_14_), channel_id=1, source_target_pairs={{0,2},{2,0},{4,6},{6,4},{8,10},{10,8},{12,14},{14,12},{1,3},{3,1},... | collective-permute-start | bytes 1572872 | tf_op jit(solution)/shard_map/ppermute | solution.py:269
  247.8 43.4 %collective-permute-start.22 = (bf16[1024,1024]{0,1:T(8,128)(2,1)}, bf16[1024,1024]{0,1:T(8,128)(2,1)}, u32[]{:S(2)}, u32[]{:S(2)}) collective-permute-start(bf16[1024,1024]{0,1:T(8,128)(2,1)} %convolution_convert_fusion.7), channel_id=1, source_target_pairs={{0,1},{1,0},{2,3},{3,2},{4,5},{5,4},{6,7},{7,6},{8,9},{9,8},{10,11... | collective-permute-start | bytes 6291464 | tf_op jit(solution)/shard_map/ppermute | solution.py:269
  324.1 44.5 %collective-permute-start.24 = (bf16[1024,1024]{0,1:T(8,128)(2,1)}, bf16[1024,1024]{0,1:T(8,128)(2,1)}, u32[]{:S(2)}, u32[]{:S(2)}) collective-permute-start(bf16[1024,1024]{0,1:T(8,128)(2,1)} %add_convert_fusion), channel_id=1, source_target_pairs={{0,1},{1,0},{2,3},{3,2},{4,5},{5,4},{6,7},{7,6},{8,9},{9,8},{10,11... | collective-permute-start | bytes 6291464 | tf_op jit(solution)/shard_map/ppermute | solution.py:269
  328.7 84.8 %collective-permute-start.23 = (bf16[1024,1024]{0,1:T(8,128)(2,1)}, bf16[1024,1024]{0,1:T(8,128)(2,1)}, u32[]{:S(2)}, u32[]{:S(2)}) collective-permute-start(bf16[1024,1024]{0,1:T(8,128)(2,1)} %fusion.35), channel_id=1, source_target_pairs={{0,1},{1,0},{2,3},{3,2},{4,5},{5,4},{6,7},{7,6},{8,9},{9,8},{10,11... | collective-permute-start | bytes 6291464 | tf_op jit(solution)/shard_map/ppermute | solution.py:269
  503.4 24.7 %collective-permute-start.26 = (bf16[512,512]{1,0:T(8,128)(2,1)S(1)}, bf16[512,512]{1,0:T(8,128)(2,1)S(1)}, u32[]{:S(2)}, u32[]{:S(2)}) collective-permute-start(bf16[512,512]{1,0:T(8,128)(2,1)S(1)} %copy-done.81), channel_id=1, source_target_pairs={{0,2},{2,0},{4,6},{6,4},{8,10},{10,8},{12,14},{14,12},{1,3},{3,1},... | collective-permute-start | bytes 1572872 | tf_op jit(solution)/shard_map/ppermute | solution.py:269
  522.0 6.8 collective-permute-start.29
  524.8 84.8 %collective-permute-start.28 = (bf16[512,512]{1,0:T(8,128)(2,1)S(1)}, bf16[512,512]{1,0:T(8,128)(2,1)S(1)}, u32[]{:S(2)}, u32[]{:S(2)}) collective-permute-start(bf16[512,512]{1,0:T(8,128)(2,1)S(1)} %copy-done.73), channel_id=1, source_target_pairs={{0,2},{2,0},{4,6},{6,4},{8,10},{10,8},{12,14},{14,12},{1,3},{3,1},... | collective-permute-start | bytes 1572872 | tf_op jit(solution)/shard_map/ppermute | solution.py:269
  524.9 111.4 %collective-permute-start.25 = (bf16[512,512]{1,0:T(8,128)(2,1)S(1)}, bf16[512,512]{1,0:T(8,128)(2,1)S(1)}, u32[]{:S(2)}, u32[]{:S(2)}) collective-permute-start(bf16[512,512]{1,0:T(8,128)(2,1)S(1)} %get-tuple-element.42), channel_id=1, source_target_pairs={{0,2},{2,0},{4,6},{6,4},{8,10},{10,8},{12,14},{14,12},{1,3},{3,1},... | collective-permute-start | bytes 1572872 | tf_op jit(solution)/shard_map/ppermute | solution.py:269
  529.1 82.1 %collective-permute-start.35 = (bf16[512,512]{1,0:T(8,128)(2,1)S(1)}, bf16[512,512]{1,0:T(8,128)(2,1)S(1)}, u32[]{:S(2)}, u32[]{:S(2)}) collective-permute-start(bf16[512,512]{1,0:T(8,128)(2,1)S(1)} %copy-done.70), channel_id=1, source_target_pairs={{0,2},{2,0},{4,6},{6,4},{8,10},{10,8},{12,14},{14,12},{1,3},{3,1},... | collective-permute-start | bytes 1572872 | tf_op jit(solution)/shard_map/ppermute | solution.py:269
  531.5 42.0 %collective-permute-start.42 = (bf16[512,512]{1,0:T(8,128)(2,1)S(1)}, bf16[512,512]{1,0:T(8,128)(2,1)S(1)}, u32[]{:S(2)}, u32[]{:S(2)}) collective-permute-start(bf16[512,512]{1,0:T(8,128)(2,1)S(1)} %add_convert_fusion.3), channel_id=1, source_target_pairs={{4,0},{6,2},{8,4},{10,6},{12,8},{14,10},{5,1},{7,3},{9,5},{11,7},{... | collective-permute-start | bytes 1572872 | tf_op jit(solution)/shard_map/ppermute | solution.py:318
  532.9 76.7 %collective-permute-start.30 = (bf16[512,512]{1,0:T(8,128)(2,1)S(1)}, bf16[512,512]{1,0:T(8,128)(2,1)S(1)}, u32[]{:S(2)}, u32[]{:S(2)}) collective-permute-start(bf16[512,512]{1,0:T(8,128)(2,1)S(1)} %add_convert_fusion.12), channel_id=1, source_target_pairs={{0,4},{2,6},{4,0},{6,2},{8,12},{10,14},{12,8},{14,10},{1,5},{3,7},... | collective-permute-start | bytes 1572872 | tf_op jit(solution)/shard_map/ppermute | solution.py:269
  573.4 46.4 %collective-permute-start.37 = (bf16[512,512]{1,0:T(8,128)(2,1)S(1)}, bf16[512,512]{1,0:T(8,128)(2,1)S(1)}, u32[]{:S(2)}, u32[]{:S(2)}) collective-permute-start(bf16[512,512]{1,0:T(8,128)(2,1)S(1)} %add_convert_fusion.7), channel_id=1, source_target_pairs={{0,8},{2,10},{4,12},{6,14},{8,0},{10,2},{12,4},{14,6},{1,9},{3,11}... | collective-permute-start | bytes 1572872 | tf_op jit(solution)/shard_map/ppermute | solution.py:269
  609.6 35.3 %collective-permute-start.34 = (bf16[512,512]{1,0:T(8,128)(2,1)}, bf16[512,512]{1,0:T(8,128)(2,1)}, u32[]{:S(2)}, u32[]{:S(2)}) collective-permute-start(bf16[512,512]{1,0:T(8,128)(2,1)} %get-tuple-element.53), channel_id=1, source_target_pairs={{0,2},{2,0},{4,6},{6,4},{8,10},{10,8},{12,14},{14,12},{1,3},{3,1},... | collective-permute-start | bytes 1572872 | tf_op jit(solution)/shard_map/ppermute | solution.py:269
  609.7 16.6 %collective-permute-start.33 = (bf16[512,512]{1,0:T(8,128)(2,1)S(1)}, bf16[512,512]{1,0:T(8,128)(2,1)S(1)}, u32[]{:S(2)}, u32[]{:S(2)}) collective-permute-start(bf16[512,512]{1,0:T(8,128)(2,1)S(1)} %add_convert_fusion.10), channel_id=1, source_target_pairs={{4,0},{6,2},{8,4},{10,6},{12,8},{14,10},{5,1},{7,3},{9,5},{11,7},{... | collective-permute-start | bytes 1572872 | tf_op jit(solution)/shard_map/ppermute | solution.py:318
  611.2 26.3 %collective-permute-start.27 = (bf16[512,512]{1,0:T(8,128)(2,1)S(1)}, bf16[512,512]{1,0:T(8,128)(2,1)S(1)}, u32[]{:S(2)}, u32[]{:S(2)}) collective-permute-start(bf16[512,512]{1,0:T(8,128)(2,1)S(1)} %add_convert_fusion.14), channel_id=1, source_target_pairs={{0,4},{2,6},{4,0},{6,2},{8,12},{10,14},{12,8},{14,10},{1,5},{3,7},... | collective-permute-start | bytes 1572872 | tf_op jit(solution)/shard_map/ppermute | solution.py:269
  619.8 17.7 %collective-permute-start.31 = (bf16[512,512]{1,0:T(8,128)(2,1)S(1)}, bf16[512,512]{1,0:T(8,128)(2,1)S(1)}, u32[]{:S(2)}, u32[]{:S(2)}) collective-permute-start(bf16[512,512]{1,0:T(8,128)(2,1)S(1)} %add_convert_fusion.11), channel_id=1, source_target_pairs={{0,8},{2,10},{4,12},{6,14},{8,0},{10,2},{12,4},{14,6},{1,9},{3,11}... | collective-permute-start | bytes 1572872 | tf_op jit(solution)/shard_map/ppermute | solution.py:269
  626.3 19.8 %collective-permute-start.40 = (bf16[512,512]{1,0:T(8,128)(2,1)}, bf16[512,512]{1,0:T(8,128)(2,1)}, u32[]{:S(2)}, u32[]{:S(2)}) collective-permute-start(bf16[512,512]{1,0:T(8,128)(2,1)} %add_convert_fusion.5), channel_id=1, source_target_pairs={{0,8},{2,10},{4,12},{6,14},{8,0},{10,2},{12,4},{14,6},{1,9},{3,11}... | collective-permute-start | bytes 1572872 | tf_op jit(solution)/shard_map/ppermute | solution.py:269
  636.3 12.2 %collective-permute-start.38 = (bf16[512,512]{1,0:T(8,128)(2,1)}, bf16[512,512]{1,0:T(8,128)(2,1)}, u32[]{:S(2)}, u32[]{:S(2)}) collective-permute-start(bf16[512,512]{1,0:T(8,128)(2,1)} %add_convert_fusion.6), channel_id=1, source_target_pairs={{0,4},{2,6},{4,0},{6,2},{8,12},{10,14},{12,8},{14,10},{1,5},{3,7},... | collective-permute-start | bytes 1572872 | tf_op jit(solution)/shard_map/ppermute | solution.py:269
  663.9 216.1 %reduce-scatter.5.cloned.1.call-start = ((), (), s32[]{:S(2)}) async-start(), calls=%async_computation.5 | async-start | bytes 12255232 | tf_op jit(solution)/shard_map/reduce_scatter | solution.py:492
  707.2 62.4 %collective-permute-start.43 = (bf16[1024,1024]{0,1:T(8,128)(2,1)S(1)}, bf16[1024,1024]{0,1:T(8,128)(2,1)S(1)}, u32[]{:S(2)}, u32[]{:S(2)}) collective-permute-start(bf16[1024,1024]{0,1:T(8,128)(2,1)S(1)} %convolution_convert_fusion.4), channel_id=1, source_target_pairs={{0,1},{1,0},{2,3},{3,2},{4,5},{5,4},{6,7},{7,6},{8,9},{9,8},{10,11... | collective-permute-start | bytes 6291464 | tf_op jit(solution)/shard_map/ppermute | solution.py:269
  707.3 64.3 %collective-permute-start.48 = (f32[256]{0:T(256)S(1)}, f32[256]{0:T(256)S(1)}, u32[]{:S(2)}, u32[]{:S(2)}) collective-permute-start(f32[256]{0:T(256)S(1)} %pad_maximum_fusion.11), channel_id=1, source_target_pairs={{0,2},{2,0},{4,6},{6,4},{8,10},{10,8},{12,14},{14,12},{1,3},{3,1},... | collective-permute-start | bytes 3080 | tf_op jit(solution)/shard_map/ppermute | solution.py:269
  771.5 28.6 %collective-permute-start.44 = (f32[2048]{0:T(1024)S(1)}, f32[2048]{0:T(1024)S(1)}, u32[]{:S(2)}, u32[]{:S(2)}) collective-permute-start(f32[2048]{0:T(1024)S(1)} %pad_maximum_fusion.10), channel_id=1, source_target_pairs={{0,2},{2,0},{4,6},{6,4},{8,10},{10,8},{12,14},{14,12},{1,3},{3,1},... | collective-permute-start | bytes 24584 | tf_op jit(solution)/shard_map/ppermute | solution.py:269
  775.4 15.8 %collective-permute-start.50 = (f32[256]{0:T(256)S(1)}, f32[256]{0:T(256)S(1)}, u32[]{:S(2)}, u32[]{:S(2)}) collective-permute-start(f32[256]{0:T(256)S(1)} %add.286), channel_id=1, source_target_pairs={{0,8},{2,10},{4,12},{6,14},{8,0},{10,2},{12,4},{14,6},{1,9},{3,11}... | collective-permute-start | bytes 3080 | tf_op jit(solution)/shard_map/ppermute | solution.py:269
  791.2 4.6 collective-permute-start.51
  804.2 4.6 collective-permute-start.46
  808.7 14.5 %collective-permute-start.47 = (f32[2048]{0:T(1024)S(1)}, f32[2048]{0:T(1024)S(1)}, u32[]{:S(2)}, u32[]{:S(2)}) collective-permute-start(f32[2048]{0:T(1024)S(1)} %add.282), channel_id=1, source_target_pairs={{0,16},{16,0},{1,17},{17,1},{2,18},{18,2},{3,19},{19,3},{4,20},{20... | collective-permute-start | bytes 24584 | tf_op jit(solution)/shard_map/ppermute | solution.py:269
  (100 other events, 2357.2 us)
Sparse Core Ops, SparseCore 0:
  10.9 57.7 all-gather.2
  71.0 101.8 all-gather.4
  664.0 83.5 reduce-scatter.2
  749.8 130.1 reduce-scatter.4

commit v2 on v0

v2 whole, which is shorter than its diff:
```python
import functools
import math

import jax
import jax.numpy as jnp
from jax import lax
from jax.experimental import pallas as pl
from jax.experimental.pallas import tpu as pltpu
from jax.sharding import PartitionSpec as P

HEAD_SIZE = 128
PROMPT = 4096
CONT_TOK = 4096
LONGEST = 1024

EPSILON = 1e-06
ROPE_BASE = 1000000.0
MASKED = -1e30
LOG2E = math.log2(math.e)
LN2 = math.log(2.0)
SCALE = 1.0 / math.sqrt(HEAD_SIZE)

BF = jnp.bfloat16
F32 = jnp.float32
NN = (((1,), (0,)), ((), ()))
NT = (((1,), (1,)), ((), ()))
TN = (((0,), (0,)), ((), ()))
MIB = 2**20


def mm(left, right, dims=NN):
    return lax.dot_general(left, right, dims, preferred_element_type=F32)


def shaped(dims, kind):
    return jax.ShapeDtypeStruct(dims, kind)


def call(kernel, name, grid, ins, outs, scratch=(), vmem=56, flops=0, moved=0, scalars=None, keep=None):
    in_specs, arrays = [], []
    for array, block, index in ins:
        arrays.append(array)
        in_specs.append(pl.BlockSpec(memory_space=pl.ANY) if block is None else pl.BlockSpec(block, index))
    lead = 0 if scalars is None else 1
    return pl.pallas_call(
        kernel,
        grid_spec=pltpu.PrefetchScalarGridSpec(
            num_scalar_prefetch=lead,
            grid=grid,
            in_specs=in_specs,
            out_specs=[pl.BlockSpec(block, index) for _, block, index in outs],
            scratch_shapes=list(scratch),
        ),
        out_shape=[shape for shape, _, _ in outs],
        input_output_aliases={a + lead: b for a, b in (keep or {}).items()},
        compiler_params=pltpu.CompilerParams(vmem_limit_bytes=vmem * MIB),
        cost_estimate=pl.CostEstimate(flops=flops, bytes_accessed=moved, transcendentals=0),
        name=name,
    )(*([] if scalars is None else [scalars]), *arrays)


def rms(values):
    return lax.rsqrt(jnp.mean(values * values, axis=-1, keepdims=True) + EPSILON)


def turn(values, cos, sin):
    return values * cos + pltpu.roll(values, HEAD_SIZE // 2, 1) * sin


def turn_back(values, cos, sin):
    return values * cos - pltpu.roll(values, HEAD_SIZE // 2, 1) * sin


def kv_kernel(heads, x_ref, gain_ref, w_ref, hgain_ref, cos_ref, sin_ref, *refs):
    normed_ref, kv_ref, lin_ref = refs[-3:]
    x = x_ref[...].astype(F32)
    normed_ref[...] = (x * rms(x) * gain_ref[...]).astype(BF)
    both = mm(normed_ref[...], w_ref[...])
    width = heads * HEAD_SIZE
    kv_ref[1] = both[:, width:].astype(BF)
    for h in range(heads):
        cols = slice(h * HEAD_SIZE, (h + 1) * HEAD_SIZE)
        lin = both[:, cols]
        lin_ref[:, cols] = lin
        kv_ref[0, :, cols] = turn(lin * rms(lin) * hgain_ref[...], cos_ref[...], sin_ref[...]).astype(BF)


def q_kernel(heads, normed_ref, w_ref, hgain_ref, cos_ref, sin_ref, q_ref, lin_ref):
    both = mm(normed_ref[...], w_ref[...])
    for h in range(heads):
        cols = slice(h * HEAD_SIZE, (h + 1) * HEAD_SIZE)
        lin = both[:, cols]
        lin_ref[:, cols] = lin
        turned = turn(lin * rms(lin) * hgain_ref[...], cos_ref[...], sin_ref[...])
        q_ref[:, cols] = (turned * (SCALE * LOG2E)).astype(BF)


def fwd_kernel(plan, idx_ref, q_ref, lo_ref, *refs):
    half, slots, halos = plan["half"], plan["slots"], plan["halos"]
    refs = list(refs)
    slot_refs = [refs.pop(0) for _ in slots]
    halo_refs = [refs.pop(0) for _ in halos]
    prior = [refs.pop(0) for _ in range(2)] if plan["carry"] else None
    if plan["last"]:
        w_ref = refs.pop(0)
        if plan["alias"]:
            refs.pop(0)
        out_ref, lse_ref, part_ref, acc, tot, part_acc = refs
    else:
        acc, tot = refs
    me, lo_first = idx_ref[0], idx_ref[1]
    rows = q_ref.shape[0]
    if prior is None:
        acc[...] = jnp.zeros_like(acc)
        tot[...] = jnp.zeros_like(tot)
    else:
        acc[...] = prior[0][...]
        tot[...] = prior[1][...]

    def add(kv_ref, mask=None):
        for g in range(2):
            cols = slice(g * HEAD_SIZE, (g + 1) * HEAD_SIZE)
            scores = mm(q_ref[:, cols], kv_ref[0], NT)
            if mask is not None:
                scores = jnp.where(mask, scores, MASKED)
            weights = jnp.exp2(scores)
            total = weights[:, :128]
            for at in range(128, weights.shape[1], 128):
                total = total + weights[:, at : at + 128]
            acc[:, cols] += mm(weights.astype(BF), kv_ref[1])
            tot[:, cols] += total

    row = lax.broadcasted_iota(jnp.int32, (rows, 1), 0)
    col = lax.broadcasted_iota(jnp.int32, (1, rows), 1)
    for d, kv_ref in zip(halos, halo_refs):
        low = lo_ref[:, :1]
        if d == 0:
            add(kv_ref, (col <= row) & (col >= low))
        else:

            @pl.when(lo_first < -(d - 1) * rows)
            def _(d=d, kv_ref=kv_ref, low=low):
                add(kv_ref, col - d * rows >= low)

    for s, kv_ref in zip(slots, slot_refs):
        if half == 1:
            add(kv_ref)
        elif s == 0:
            add(kv_ref, col <= row)
        else:

            @pl.when(jnp.bitwise_xor(me, s) < me)
            def _(kv_ref=kv_ref):
                add(kv_ref)

    if plan["last"]:
        step, steps = pl.program_id(0), pl.num_programs(0)
        for g in range(2):
            cols = slice(g * HEAD_SIZE, (g + 1) * HEAD_SIZE)
            total = jnp.sum(tot[:, cols], axis=1, keepdims=True)
            out_ref[:, cols] = (acc[:, cols] / total).astype(BF)
            lse_ref[0, g : g + 1, :] = jnp.log2(jnp.sum(tot[:, cols].T, axis=0, keepdims=True))
        part = mm(out_ref[...], w_ref[...], NT)

        @pl.when(step == 0)
        def _():
            part_acc[...] = part

        @pl.when(step > 0)
        def _():
            part_acc[...] += part

        @pl.when(step == steps - 1)
        def _():
            part_ref[...] = part_acc[...].astype(BF)


def attention_forward(half, scalars, q, low, slots, halos, carry=None, last=None):
    rows, heads = q.shape[0] // 2, q.shape[1] // 256
    plan = dict(half=half, slots=list(slots), halos=list(halos), carry=carry is not None,
                last=last is not None, alias=last is not None and last[1] is not None)
    mine = lambda h, i: (half, h)
    part = lambda h, i: (0, h)
    ins = [(q, (rows, 256), mine), (low, (rows, 128), lambda h, i: (0, 0))]
    for kv in list(slots.values()) + list(halos.values()):
        ins.append((kv, (2, rows, 128), lambda h, i: (0, 0, h)))
    if carry is not None:
        ins += [(c, (rows, 256), part) for c in carry]
    scratch, keep = [], {}
    state = shaped((rows, heads * 256), F32)
    if last is None:
        outs = [(state, (rows, 256), part)] * 2
    else:
        w_rest, other = last
        model = w_rest.shape[0]
        ins.append((w_rest, (model, 256), part))
        if other is not None:
            keep = {len(ins): 0}
            ins.append((other, None, None))
        outs = [
            (shaped((2 * rows, heads * 256), BF), (rows, 256), mine),
            (shaped((heads, 8, rows), F32), (1, 8, rows), lambda h, i: (h, 0, 0)),
            (shaped((rows, model), BF), (rows, model), lambda h, i: (0, 0)),
        ]
        scratch = [pltpu.VMEM((rows, 256), F32)] * 2 + [pltpu.VMEM((rows, model), F32)]
    blocks = len(slots) * (2 if half else 1) + len(halos)
    pairs = heads * rows * rows * blocks
    return call(functools.partial(fwd_kernel, plan), "attend", (heads,), ins, outs, scratch,
                flops=pairs * 1024, moved=8 * MIB, scalars=scalars, keep=keep)


def bwd_kernel(plan, idx_ref, q_ref, do_ref, lse_ref, delta_ref, lo_ref, *refs):
    half, slots, halos = plan["half"], plan["slots"], plan["halos"]
    refs = list(refs)
    slot_refs = [refs.pop(0) for _ in slots]
    halo_refs = [refs.pop(0) for _ in halos]
    prior_dq = refs.pop(0) if plan["carry"] else None
    prior = [refs.pop(0) for _ in slots] if plan["sum"] else None
    dq_ref = refs.pop(0)
    slot_outs = [refs.pop(0) for _ in slots]
    halo_outs = [refs.pop(0) for _ in halos]
    qs, dos, lses, deltas, dq = refs
    me, lo_first = idx_ref[0], idx_ref[1]
    rows = q_ref.shape[0]
    for g in range(2):
        cols, at = slice(g * HEAD_SIZE, (g + 1) * HEAD_SIZE), slice(g * rows, (g + 1) * rows)
        qs[at, :] = q_ref[:, cols]
        dos[at, :] = do_ref[:, cols]
        lses[:, at] = lse_ref[0, g : g + 1, :]
        deltas[:, at] = delta_ref[0, g : g + 1, :]
    dq[...] = jnp.zeros_like(dq) if prior_dq is None else prior_dq[...]

    def block(kv_ref, out_ref, mask=None, before=None):
        keys = kv_ref[0]
        scores = mm(keys, qs[...], NT)
        dp = mm(kv_ref[1], dos[...], NT)
        scores = scores - lses[...]
        if mask is not None:
            scores = jnp.where(mask, scores, MASKED)
        probs = jnp.exp2(scores)
        ds = (probs * (dp - deltas[...])).astype(BF)
        dq[...] += mm(keys.T, ds)
        dk, dv = mm(ds, qs[...]) * LN2, mm(probs.astype(BF), dos[...])
        if before is not None:
            dk, dv = dk + before[0].astype(F32), dv + before[1].astype(F32)
        out_ref[0] = dk.astype(BF)
        out_ref[1] = dv.astype(BF)

    lane = lax.broadcasted_iota(jnp.int32, (1, 2 * rows), 1)
    lane = jnp.where(lane >= rows, lane - rows, lane)
    key = lax.broadcasted_iota(jnp.int32, (rows, 1), 0)

    def when(needed, kv_ref, out_ref, mask=None):
        @pl.when(needed)
        def _():
            block(kv_ref, out_ref, mask)

        @pl.when(jnp.logical_not(needed))
        def _():
            out_ref[...] = jnp.zeros_like(out_ref)

    low = lo_ref[:1, :]
    for d, kv_ref, out_ref in zip(halos, halo_refs, halo_outs):
        if d == 0:
            block(kv_ref, out_ref, (key <= lane) & (key >= low))
        else:
            when(lo_first < -(d - 1) * rows, kv_ref, out_ref, key - d * rows >= low)
    for at, (s, kv_ref, out_ref) in enumerate(zip(slots, slot_refs, slot_outs)):
        if half == 1:
            block(kv_ref, out_ref, None, prior[at])
        elif s == 0:
            block(kv_ref, out_ref, key <= lane)
        else:
            when(jnp.bitwise_xor(me, s) < me, kv_ref, out_ref)
    if plan["last"]:
        for g in range(2):
            cols = slice(g * HEAD_SIZE, (g + 1) * HEAD_SIZE)
            dq_ref[:, cols] = dq[:, g * rows : (g + 1) * rows].T * SCALE
    else:
        dq_ref[...] = dq[...]


def attention_backward(half, scalars, q, do, lse, delta, low, slots, halos, carry=None, prior=None, last=True):
    rows, heads = q.shape[0] // 2, q.shape[1] // 256
    plan = dict(half=half, slots=list(slots), halos=list(halos), carry=carry is not None,
                sum=prior is not None, last=last)
    part = lambda h, i: (0, h)
    stat = lambda h, i: (h, 0, 0)
    kv_map = lambda h, i: (0, 0, h)
    ins = [
        (q, (rows, 256), lambda h, i: (half, h)),
        (do, (rows, 256), part),
        (lse, (1, 8, rows), stat),
        (delta, (1, 8, rows), stat),
        (low, (8, 2 * rows), lambda h, i: (0, 0)),
    ]
    pieces = list(slots.values()) + list(halos.values())
    ins += [(kv, (2, rows, 128), kv_map) for kv in pieces]
    if carry is not None:
        ins.append((carry, (128, 2 * rows), lambda h, i: (h, 0)))
    if prior is not None:
        ins += [(prior[s], (2, rows, 128), kv_map) for s in slots]
    if last:
        outs = [(shaped((rows, heads * 256), F32), (rows, 256), part)]
    else:
        outs = [(shaped((heads * 128, 2 * rows), F32), (128, 2 * rows), lambda h, i: (h, 0))]
    outs += [(shaped(kv.shape, BF), (2, rows, 128), kv_map) for kv in pieces]
    scratch = [
        pltpu.VMEM((2 * rows, 128), BF),
        pltpu.VMEM((2 * rows, 128), BF),
        pltpu.VMEM((1, 2 * rows), F32),
        pltpu.VMEM((1, 2 * rows), F32),
        pltpu.VMEM((128, 2 * rows), F32),
    ]
    blocks = len(slots) * (2 if half else 1) + len(halos)
    pairs = heads * rows * rows * blocks
    results = call(functools.partial(bwd_kernel, plan), "attend_back", (heads,), ins, outs, scratch,
                   flops=pairs * 2560, moved=8 * MIB, scalars=scalars)
    n = len(slots)
    return results[0], dict(zip(slots, results[1 : 1 + n])), dict(zip(halos, results[1 + n :]))


def ffn_kernel(x_ref, own_ref, got_ref, gain_ref, dy_ref, gu_ref, down_ref, *refs):
    resid_ref, normed_ref, hidden_ref, dgu_ref, out_ref, back_ref, normed, out_acc, back_acc = refs[-9:]
    step, steps = pl.program_id(0), pl.num_programs(0)

    @pl.when(step == 0)
    def _():
        resid = x_ref[...].astype(F32) + (own_ref[...].astype(F32) + got_ref[...].astype(F32))
        resid_ref[...] = resid
        normed[...] = (resid * rms(resid) * gain_ref[...]).astype(BF)
        normed_ref[...] = normed[...]
        out_acc[...] = jnp.zeros_like(out_acc)
        back_acc[...] = jnp.zeros_like(back_acc)

    wide = down_ref.shape[1]
    both = mm(normed[...], gu_ref[...])
    d_hidden = mm(dy_ref[...], down_ref[...])
    gate, up = both[:, :wide], both[:, wide:]
    sig = 1.0 / (1.0 + jnp.exp(-gate))
    silu = gate * sig
    hidden = (silu * up).astype(BF)
    hidden_ref[...] = hidden
    d_up = (d_hidden * silu).astype(BF)
    d_gate = (d_hidden * up * (sig + silu * (1.0 - sig))).astype(BF)
    dgu_ref[:, :wide] = d_gate
    dgu_ref[:, wide:] = d_up
    out_acc[...] += mm(hidden, down_ref[...], NT)
    back_acc[...] += mm(dgu_ref[...], gu_ref[...], NT)

    @pl.when(step == steps - 1)
    def _():
        out_ref[...] = out_acc[...].astype(BF)
        back_ref[...] = back_acc[...].astype(BF)


def feed_forward(half, x, own, got, gain, dy, w_rest, o_cols, chunk, whole=None):
    rows, model = own.shape
    units = (w_rest.shape[1] - o_cols) // 3
    steps = units // chunk
    mine, once = lambda f: (half, 0), lambda f: (0, 0)
    at_gu, at_down = o_cols // (2 * chunk), (o_cols + 2 * units) // chunk
    block = (rows, model)
    ins = [
        (x, block, mine), (own, block, once), (got, block, once), (gain, (1, model), once), (dy, block, mine),
        (w_rest, (model, 2 * chunk), lambda f: (0, at_gu + f)),
        (w_rest, (model, chunk), lambda f: (0, at_down + f)),
    ]
    keep = {}
    if whole is not None:
        keep = {len(ins) + i: 1 + i for i in range(3)}
        ins += [(array, None, None) for array in whole]
    outs = [
        (shaped((rows, model), F32), block, once),
        (shaped((2 * rows, model), BF), block, mine),
        (shaped((2 * rows, units), BF), (rows, chunk), lambda f: (half, f)),
        (shaped((2 * rows, 2 * units), BF), (rows, 2 * chunk), lambda f: (half, f)),
        (shaped((rows, model), BF), block, once),
        (shaped((rows, model), BF), block, once),
    ]
    scratch = [pltpu.VMEM(block, BF), pltpu.VMEM(block, F32), pltpu.VMEM(block, F32)]
    return call(ffn_kernel, "feed_forward", (steps,), ins, outs, scratch,
                flops=12 * rows * model * units, moved=20 * MIB, keep=keep)


def norm_back(grad, values, gain):
    scale = rms(values)
    unit = values * scale
    inner = grad * gain
    return scale * (inner - unit * jnp.mean(inner * unit, axis=-1, keepdims=True)), grad * unit


def mixed_kernel(heads, own_ref, got_ref, resid_ref, gain_ref, dy_ref, w_ref, att_ref, *refs):
    d_resid_ref, mixed_ref, datt_ref, delta_ref, dgain_ref = refs[-5:]
    grad = own_ref[...].astype(F32) + got_ref[...].astype(F32)
    d_norm, summand = norm_back(grad, resid_ref[...], gain_ref[...])
    dgain_ref[...] = jnp.sum(summand, axis=0, keepdims=True)
    d_resid = dy_ref[...].astype(F32) + d_norm
    d_resid_ref[...] = d_resid
    mixed_ref[...] = d_resid.astype(BF)
    datt_ref[...] = mm(mixed_ref[...], w_ref[...]).astype(BF)
    for h in range(heads):
        cols = slice(h * HEAD_SIZE, (h + 1) * HEAD_SIZE)
        product = datt_ref[:, cols].astype(F32) * att_ref[:, cols].astype(F32)
        delta_ref[h // 2, h % 2 : h % 2 + 1, :] = jnp.sum(product.T, axis=0, keepdims=True)


def mixed_back(half, own, got, resid, gain, dy, w_rest, o_cols, attended, whole=None):
    rows, model = own.shape
    heads = o_cols // HEAD_SIZE
    mine, once = lambda f: (half, 0), lambda f: (0, 0)
    block = (rows, model)
    ins = [
        (own, block, once), (got, block, once), (resid, block, once), (gain, (1, model), once),
        (dy, block, mine), (w_rest, (model, o_cols), once), (attended, (rows, o_cols), mine),
    ]
    keep = {}
    if whole is not None:
        keep = {len(ins): 1}
        ins.append((whole, None, None))
    outs = [
        (shaped((rows, model), F32), block, once),
        (shaped((2 * rows, model), BF), block, mine),
        (shaped((rows, o_cols), BF), (rows, o_cols), once),
        (shaped((heads // 2, 8, rows), F32), (heads // 2, 8, rows), lambda f: (0, 0, 0)),
        (shaped((1, model), F32), (1, model), once),
    ]
    return call(functools.partial(mixed_kernel, heads), "mixed_back", (1,), ins, outs,
                flops=2 * rows * model * o_cols, moved=12 * MIB, keep=keep)


def qkv_kernel(heads, kv_heads, n_kv, dq_ref, ql_ref, kl_ref, qg_ref, kg_ref, cos_ref, sin_ref, w_ref, *refs):
    kv_refs = refs[:n_kv]
    dqkv_ref, part_ref, gains_ref = refs[-3:]
    cos, sin = cos_ref[...], sin_ref[...]
    q_cols, k_cols = heads * HEAD_SIZE, kv_heads * HEAD_SIZE

    def total(which, cols):
        value = kv_refs[0][which, :, cols].astype(F32)
        for ref in kv_refs[1:]:
            value = value + ref[which, :, cols].astype(F32)
        return value

    q_sum = k_sum = jnp.zeros((1, HEAD_SIZE), F32)
    for h in range(heads):
        cols = slice(h * HEAD_SIZE, (h + 1) * HEAD_SIZE)
        grad, summand = norm_back(turn_back(dq_ref[:, cols], cos, sin), ql_ref[:, cols], qg_ref[...])
        dqkv_ref[:, cols] = grad.astype(BF)
        q_sum = q_sum + jnp.sum(summand, axis=0, keepdims=True)
    for h in range(kv_heads):
        cols = slice(h * HEAD_SIZE, (h + 1) * HEAD_SIZE)
        grad, summand = norm_back(turn_back(total(0, cols), cos, sin), kl_ref[:, cols], kg_ref[...])
        dqkv_ref[:, q_cols + h * HEAD_SIZE : q_cols + (h + 1) * HEAD_SIZE] = grad.astype(BF)
        k_sum = k_sum + jnp.sum(summand, axis=0, keepdims=True)
    dqkv_ref[:, q_cols + k_cols :] = total(1, slice(None)).astype(BF)
    part_ref[...] = mm(dqkv_ref[...], w_ref[...], NT).astype(BF)
    gains_ref[:, :HEAD_SIZE] = q_sum
    gains_ref[:, HEAD_SIZE:] = k_sum


def qkv_back(half, dq, q_lin, k_lin, q_gain, k_gain, cos, sin, w_qkv, kvs, whole=None):
    rows, q_cols = dq.shape
    k_cols = k_lin.shape[1]
    model, cols = w_qkv.shape
    mine, once = lambda f: (half, 0), lambda f: (0, 0)
    ins = [
        (dq, (rows, q_cols), once), (q_lin, (rows, q_cols), mine), (k_lin, (rows, k_cols), once),
        (q_gain, (1, HEAD_SIZE), once), (k_gain, (1, HEAD_SIZE), once),
        (cos, (rows, HEAD_SIZE), mine), (sin, (rows, HEAD_SIZE), mine), (w_qkv, (model, cols), once),
    ]
    ins += [(kv, (2, rows, k_cols), lambda f: (0, 0, 0)) for kv in kvs]
    keep = {}
    if whole is not None:
        keep = {len(ins): 0}
        ins.append((whole, None, None))
    outs = [
        (shaped((2 * rows, cols), BF), (rows, cols), mine),
        (shaped((rows, model), BF), (rows, model), once),
        (shaped((1, 2 * HEAD_SIZE), F32), (1, 2 * HEAD_SIZE), once),
    ]
    kernel = functools.partial(qkv_kernel, q_cols // HEAD_SIZE, k_cols // HEAD_SIZE, len(kvs))
    return call(kernel, "qkv_back", (1,), ins, outs, flops=2 * rows * model * cols, moved=16 * MIB, keep=keep)


def tokens_kernel(own_ref, got_ref, x_ref, gain_ref, d_resid_ref, *refs):
    out_ref, dgain_ref = refs[-2:]
    grad = own_ref[...].astype(F32) + got_ref[...].astype(F32)
    d_norm, summand = norm_back(grad, x_ref[...].astype(F32), gain_ref[...])
    dgain_ref[...] = jnp.sum(summand, axis=0, keepdims=True)
    out_ref[...] = (d_resid_ref[...] + d_norm).astype(BF)


def tokens_back(half, own, got, x, gain, d_resid, whole=None):
    rows, model = own.shape
    mine, once = lambda f: (half, 0), lambda f: (0, 0)
    block = (rows, model)
    ins = [(own, block, once), (got, block, once), (x, block, mine), (gain, (1, model), once), (d_resid, block, once)]
    keep = {}
    if whole is not None:
        keep = {len(ins): 0}
        ins.append((whole, None, None))
    outs = [(shaped((2 * rows, model), BF), block, mine), (shaped((1, model), F32), (1, model), once)]
    return call(tokens_kernel, "tokens_back", (1,), ins, outs, flops=rows * model * 10, moved=8 * MIB, keep=keep)


def swap(value, axis, bit):
    size = lax.axis_size(axis)
    return lax.ppermute(value, axis, [(i, i ^ bit) for i in range(size)])


def shift(value, by):
    size = lax.axis_size("ctx")
    return lax.ppermute(value, "ctx", [(i, i + by) for i in range(size) if 0 <= i + by < size])


def add_low(left, right):
    return (left.astype(F32) + right.astype(F32)).astype(BF)


def butterfly(value, axes):
    for axis in axes:
        bit = 1
        while bit < lax.axis_size(axis):
            value = value + swap(value, axis, bit)
            bit *= 2
    return value


def after(value, *others):
    return lax.optimization_barrier((value, *others))[0]


def rotary_tables(position):
    half_dim = HEAD_SIZE // 2
    inverse_freq = jnp.exp(jnp.arange(half_dim, dtype=F32) * (-math.log(ROPE_BASE) / half_dim))
    angles = position.astype(F32)[:, None] * inverse_freq[None, :]
    cosine, sine = jnp.cos(angles), jnp.sin(angles)
    return jnp.concatenate([cosine, cosine], axis=-1), jnp.concatenate([-sine, sine], axis=-1)


def body(
    tokens,
    cont_lengths,
    attn_gain,
    ffn_gain,
    query_gain,
    key_gain,
    w_query,
    key_weight,
    value_weight,
    w_out,
    w_gate,
    w_up,
    w_down,
    cotangent,
):
    ctx_size = lax.axis_size("ctx")
    weight_axes = ("shard", "ctx")
    parts = lax.axis_size("shard") * ctx_size
    me = lax.axis_index("ctx")
    part = lax.axis_index("shard") * ctx_size + me
    rows, model = tokens.shape[0] // 2, tokens.shape[1]
    n_halo = 1 + -(-(LONGEST - 1) // rows)
    lengths = cont_lengths[0]

    gains = jnp.concatenate([attn_gain, ffn_gain, query_gain, key_gain])[None]
    spread = jnp.where(jnp.arange(parts)[:, None] == part, gains, jnp.zeros((), BF))
    gains = butterfly(spread, ("ctx", "shard")).astype(F32)
    wide, narrow = attn_gain.shape[0], query_gain.shape[0]
    gain_one = gains[:, :wide].reshape(1, -1)
    gain_two = gains[:, wide : 2 * wide].reshape(1, -1)
    gain_q = gains[:, 2 * wide : 2 * wide + narrow].reshape(1, -1)
    gain_k = gains[:, 2 * wide + narrow :].reshape(1, -1)
    q_cols, k_cols = w_query.shape[1], key_weight.shape[1]
    o_cols, units = w_out.shape[0], w_gate.shape[1]
    heads, kv_heads = q_cols // HEAD_SIZE, k_cols // HEAD_SIZE
    chunk = math.gcd(units, 512)
    w_qkv = lax.all_gather(
        jnp.concatenate([w_query, key_weight, value_weight], axis=1), weight_axes, axis=0, tiled=True
    )
    pieces = [w_out.T]
    for at in range(0, units, chunk):
        pieces += [w_gate[:, at : at + chunk], w_up[:, at : at + chunk]]
    w_rest = lax.all_gather(jnp.concatenate(pieces + [w_down.T], axis=1), weight_axes, axis=0, tiled=True)

    cont_at = me * rows + jnp.arange(rows, dtype=jnp.int32)
    cont_ends = jnp.cumsum(lengths)
    starts = cont_ends - lengths
    seg = jnp.sum((cont_ends[None, :] <= cont_at[:, None]).astype(jnp.int32), axis=1)
    numbers = jnp.arange(lengths.shape[0], dtype=jnp.int32)
    first = jnp.sum(jnp.where(numbers[None, :] == seg[:, None], starts[None, :], 0), axis=1)
    position = jnp.concatenate([me * rows + jnp.arange(rows, dtype=jnp.int32), PROMPT + cont_at - first])
    low = first - me * rows
    low_col = jnp.broadcast_to(low[:, None], (rows, 128))
    low_row = jnp.broadcast_to(jnp.concatenate([low, low])[None, :], (8, 2 * rows))
    scalars = jnp.stack([me, low[0]])
    cos, sin = rotary_tables(position)

    once = lambda f: (0, 0)

    def keys_values(half, whole=None):
        mine = lambda f: (half, 0)
        ins = [
            (tokens, (rows, model), mine), (gain_one, (1, model), once),
            (w_qkv, (model, 2 * k_cols), lambda f: (0, q_cols // (2 * k_cols))),
            (gain_k, (1, HEAD_SIZE), once), (cos, (rows, HEAD_SIZE), mine), (sin, (rows, HEAD_SIZE), mine),
        ]
        keep = {}
        if whole is not None:
            keep = {len(ins): 0}
            ins.append((whole, None, None))
        outs = [
            (shaped((2 * rows, model), BF), (rows, model), mine),
            (shaped((2, rows, k_cols), BF), (2, rows, k_cols), lambda f: (0, 0, 0)),
            (shaped((rows, k_cols), F32), (rows, k_cols), once),
        ]
        return call(functools.partial(kv_kernel, kv_heads), "keys_values", (1,), ins, outs,
                    flops=4 * rows * model * k_cols, moved=8 * MIB, keep=keep)

    normed, kv_p, k_lin_p = keys_values(0)
    slots = {0: kv_p}
    if ctx_size == 8:
        slots[2], slots[4] = swap(kv_p, "ctx", 2), swap(kv_p, "ctx", 4)
        slots[1] = swap(kv_p, "ctx", 1)
    normed, kv_c, k_lin_c = keys_values(1, normed)
    halos = {0: kv_c}
    odd = (me % 2) == 1
    if ctx_size == 8:
        halos[2] = shift(kv_c, 2)
        slots[6] = jnp.stack([swap(slots[4][0], "ctx", 2), swap(slots[2][1], "ctx", 4)])
        slots[3], slots[5], slots[7] = (swap(slots[s], "ctx", 1) for s in (2, 4, 6))
        halos[1] = swap(jnp.where(odd, halos[2], kv_c), "ctx", 1)
    else:
        both, bit = kv_p[None], 1
        while bit < ctx_size:
            both = jnp.concatenate([both, swap(both, "ctx", bit)])
            bit *= 2
        slots = {s: both[s] for s in range(ctx_size)}
        halos.update({d: shift(kv_c, d) for d in range(1, n_halo)})

    def pick(source, wanted):
        return {s: source[s] for s in source if s in wanted}

    mine = lambda f: (f, 0)
    q, q_lin = call(
        functools.partial(q_kernel, heads), "queries", (2,),
        [
            (normed, (rows, model), mine), (w_qkv, (model, q_cols), lambda f: (0, 0)),
            (gain_q, (1, HEAD_SIZE), lambda f: (0, 0)),
            (cos, (rows, HEAD_SIZE), mine), (sin, (rows, HEAD_SIZE), mine),
        ],
        [(shaped((2 * rows, q_cols), BF), (rows, q_cols), mine), (shaped((2 * rows, q_cols), F32), (rows, q_cols), mine)],
        flops=4 * rows * model * q_cols, moved=12 * MIB,
    )

    near, middle, far = (0, 1), (2, 3, 4, 5), tuple(range(6, ctx_size))
    p_state = attention_forward(0, scalars, q, low_col, pick(slots, near), {})
    c_state = attention_forward(1, scalars, q, low_col, pick(slots, near), pick(halos, (0,)))
    c_state = attention_forward(1, scalars, q, low_col, pick(slots, middle), {}, c_state)
    attended, lse_p, part_p = attention_forward(
        0, scalars, q, low_col, pick(slots, middle + far), {}, p_state, (w_rest, None)
    )
    got_p = swap(part_p, "tensor", 1)
    attended, lse_c, part_c = attention_forward(
        1, scalars, q, low_col, pick(slots, far), pick(halos, range(1, n_halo)), c_state, (w_rest, attended)
    )
    got_c = swap(part_c, "tensor", 1)

    resid_p, *whole, out_p, back_p = feed_forward(
        0, tokens, part_p, got_p, gain_two, cotangent, w_rest, o_cols, chunk
    )
    back_got_p = swap(back_p, "tensor", 1)
    resid_c, *whole, out_c, back_c = feed_forward(
        1, tokens, part_c, got_c, gain_two, cotangent, w_rest, o_cols, chunk, whole
    )
    back_got_c = swap(back_c, "tensor", 1)
    normed_ffn, hidden, d_gu = whole
    ffn_grads = jnp.concatenate(
        [mm(normed_ffn, d_gu, TN).astype(BF), mm(cotangent, hidden, TN).astype(BF)], axis=1
    )
    ffn_share = lax.psum_scatter(ffn_grads, weight_axes, scatter_dimension=0, tiled=True)

    back_got_p = after(back_got_p, ffn_grads)
    d_resid_p, d_mixed, d_att_p, delta_p, d_two_p = mixed_back(
        0, back_p, back_got_p, resid_p, gain_two, cotangent, w_rest, o_cols, attended
    )
    dq_p, from_p, _ = attention_backward(0, scalars, q, d_att_p, lse_p, delta_p, low_row, slots, {})
    d_resid_c, d_mixed, d_att_c, delta_c, d_two_c = mixed_back(
        1, back_c, back_got_c, resid_c, gain_two, cotangent, w_rest, o_cols, attended, d_mixed
    )
    out_grad = mm(d_mixed, attended, TN).astype(BF)
    out_share = lax.psum_scatter(out_grad, weight_axes, scatter_dimension=0, tiled=True)
    c_args = (scalars, q, d_att_c, lse_c, delta_c, low_row)
    dq_c, g, g_halo = attention_backward(1, *c_args, pick(slots, far), halos, None, pick(from_p, far), False)
    dq_c, more, _ = attention_backward(1, *c_args, pick(slots, middle), {}, dq_c, pick(from_p, middle), False)
    g.update(more)
    dq_c, more, _ = attention_backward(1, *c_args, pick(slots, near), {}, dq_c, pick(from_p, near), True)
    g.update(more)

    if ctx_size == 8:
        g6 = add_low(g[6], swap(g[7], "ctx", 1))
        k6, v6 = swap(g6[0], "ctx", 2), swap(g6[1], "ctx", 4)
        g4, g2 = add_low(g[4], swap(g[5], "ctx", 1)), add_low(g[2], swap(g[3], "ctx", 1))
        g4 = jnp.stack([add_low(g4[0], k6), g4[1]])
        g2 = jnp.stack([g2[0], add_low(g2[1], v6)])
        kvs_p = [g[0], swap(g[1], "ctx", 1), swap(g2, "ctx", 2), swap(g4, "ctx", 4)]
        zero = jnp.zeros((), BF)
        near_one = swap(g_halo[1], "ctx", 1)
        two = shift(add_low(g_halo[2], jnp.where(odd, near_one, zero)), -2)
        kvs_c = [g_halo[0], jnp.where(odd, zero, near_one), two]
    else:
        both = jnp.stack([g[s] for s in range(ctx_size)])
        while both.shape[0] > 1:
            size = both.shape[0] // 2
            both = add_low(both[:size], swap(both[size:], "ctx", size))
        kvs_p = [both[0]]
        kvs_c = [g_halo[0]] + [shift(g_halo[d], -d) for d in range(1, n_halo)]

    d_qkv, into_c, heads_c = qkv_back(1, dq_c, q_lin, k_lin_c, gain_q, gain_k, cos, sin, w_qkv, kvs_c)
    into_got_c = swap(into_c, "tensor", 1)
    d_qkv, into_p, heads_p = qkv_back(0, dq_p, q_lin, k_lin_p, gain_q, gain_k, cos, sin, w_qkv, kvs_p, d_qkv)
    into_got_p = swap(into_p, "tensor", 1)
    qkv_grad = mm(normed, d_qkv, TN).astype(BF)
    qkv_share = lax.psum_scatter(qkv_grad, weight_axes, scatter_dimension=0, tiled=True)
    grad_tokens, d_one_c = tokens_back(1, into_c, into_got_c, tokens, gain_one, d_resid_c)
    grad_tokens, d_one_p = tokens_back(0, into_p, into_got_p, tokens, gain_one, d_resid_p, grad_tokens)

    out_p, out_c = after(out_p, dq_p), after(out_c, dq_p)
    layer_out = jnp.concatenate(
        [
            (resid + (own.astype(F32) + swap(own, "tensor", 1).astype(F32))).astype(BF)
            for resid, own in ((resid_p, out_p), (resid_c, out_c))
        ]
    )

    model_gains = jnp.concatenate([d_one_c + d_one_p, d_two_c + d_two_p])
    model_gains = butterfly(model_gains, ("ctx", "shard")).reshape(2, parts, wide)
    head_gains = butterfly(heads_c + heads_p, ("ctx", "shard", "tensor")).reshape(2, parts, narrow)
    model_gains = lax.dynamic_index_in_dim(model_gains, part, 1, keepdims=False)
    head_gains = lax.dynamic_index_in_dim(head_gains, part, 1, keepdims=False)

    qkv_share, ffn_share, out_share = (s.astype(F32) for s in (qkv_share, ffn_share, out_share))
    gate_up = ffn_share[:, : 2 * units].reshape(wide, units // chunk, 2, chunk)
    return (
        layer_out,
        grad_tokens,
        model_gains[0],
        model_gains[1],
        head_gains[0],
        head_gains[1],
        qkv_share[:, :q_cols],
        qkv_share[:, q_cols : q_cols + k_cols],
        qkv_share[:, q_cols + k_cols :],
        out_share.T,
        gate_up[:, :, 0].reshape(wide, units),
        gate_up[:, :, 1].reshape(wide, units),
        ffn_share[:, 2 * units :].T,
    )


def solution(mesh):
    split = ("shard", "ctx")
    rows, gain = P(split, None), P(split)
    into, out_of = P(split, "tensor"), P("tensor", split)
    in_specs = (rows, P("shard", None)) + (gain,) * 4 + (into,) * 3 + (out_of,)
    in_specs += (into, into, out_of, rows)
    out_specs = (rows, rows) + (gain,) * 4 + (into,) * 3 + (out_of, into, into, out_of)
    return jax.shard_map(body, mesh=mesh, in_specs=in_specs, out_specs=out_specs, check_vma=False)
```

time: 2350 us -> 785 us (0.33)
  matrix products: 906 us -> 25.4 us
  waiting for transfers between devices: 1010 us -> 285 us
  Pallas kernels: 0 us -> 243 us
  starting transfers between devices: 1.05 us -> 149 us
  other arithmetic: 152 us -> 28.3 us
  blocking collectives: 110 us -> 0 us
  local copies, waits for them, and re-layouts: 132 us -> 32.8 us
    dot_general x63 -> x4, matrix products: 906 us -> 25.4 us  [mm(): return lax.dot_general(left, right, dims, preferred_element_type=F32)]
    reduce_scatter x9 -> x3, waiting for transfers between devices: 615 us -> 52.3 us  [the longest x1 52.3 us: body(): lax.psum_scatter(ffn_grads, weight_axes, scatter_dimension=0, tiled=True)]
    pallas_call x0 -> x20, Pallas kernels: none -> 243 us  [call(): pl.pallas_call(kernel, grid_spec=pltpu.PrefetchScalarGridSpec(num_scalar_...]
    ppermute x0 -> x41, waiting for transfers between devices: none -> 196 us  [the longest x39 196 us: swap(): return lax.ppermute(value, axis, [(i, i ^ bit) for i in range(size)])]
    all_gather x9 -> x2, waiting for transfers between devices: 217 us -> 36.7 us  [the longest x1 35.7 us: body(): lax.all_gather(jnp.concatenate([w_query, key_weight, value_weight], axis=...]
    psum x3 -> x0, waiting for transfers between devices: 177 us -> none  [the longest x1 62.5 us: body(): lax.psum(ffn_back_part.astype(jnp.bfloat16), 'tensor').astype(jnp.float32)]
    ppermute x0 -> x41, starting transfers between devices: none -> 149 us  [the longest x39 144 us: swap(): return lax.ppermute(value, axis, [(i, i ^ bit) for i in range(size)])]
    unnamed x2 -> x0, blocking collectives: 105 us -> none
  transfers between devices with their start and end apart: 21 -> 46, of which waited for: 18 -> 20; matrix products, arithmetic and copies ran while one was open for 18% -> 9% of each run, Pallas kernels for 0% -> 26%
where the time goes in v2:
time: 785 us; the launch traced here: 779 us
  waiting for transfers between devices  285 us (36%)
  Pallas kernels  243 us (31%)
  starting transfers between devices  149 us (19%)
  local copies, waits for them, and re-layouts  32.8 us (4%)
  other arithmetic  28.3 us (4%)
  matrix products  25.4 us (3%)
  between operations  14.8 us (2%)
    pallas_call x20, Pallas kernels, call(): pl.pallas_call(kernel, grid_spec=pltpu.PrefetchScalarGridSpec(num_scalar_...  243 us
    ppermute x39, waiting for transfers between devices, swap(): return lax.ppermute(value, axis, [(i, i ^ bit) for i in range(size)])  196 us
    ppermute x39, starting transfers between devices, swap(): return lax.ppermute(value, axis, [(i, i ^ bit) for i in range(size)])  144 us
    reduce_scatter x1, waiting for transfers between devices, body(): lax.psum_scatter(ffn_grads, weight_axes, scatter_dimension=0, tiled=True)  52.3 us
    all_gather x1, waiting for transfers between devices, body(): lax.all_gather(jnp.concatenate([w_query, key_weight, value_weight], axis=...  35.7 us
    dot_general x4, matrix products, mm(): return lax.dot_general(left, right, dims, preferred_element_type=F32)  25.4 us
    unnamed x83, local copies, waits for them, and re-layouts  16.7 us
  transfers between devices with their start and end apart: 46, of which 20 were waited for; matrix products, arithmetic and copies ran while one was open for 9% of the time, Pallas kernels for 26%

profile of v2, /device:TPU:0, one launch (start us, length us, event | category | flops | bytes accessed | tf_op | source)
XLA Modules:
  0.0 778.6 jit_solution(6464061216913586400)
XLA Ops:
  18.5 2.8 collective-permute-start.1
  27.0 2.8 collective-permute-start.3
  33.1 35.7 %all-gather.3.cloned.1.call-done.w_ref = bf16[1024,2048]{1,0:T(8,128)(2,1)} async-done(((bf16[64,2048]{1,0:T(8,128)(2,1)}), bf16[1024,2048]{1,0:T(8,128)(2,1)}) %all-gather.3.cloned.1.call-update) | async-done | bytes 4194320 | tf_op jit(solution)/shard_map/all_gather | solution.py:578
  68.8 5.6 keys_values.2
  77.3 5.9 keys_values.3
  83.2 3.0 collective-permute-start.14
  86.2 25.4 %collective-permute-done.5.refs_1_.refs_2_ = bf16[2,512,512]{2,1,0:T(8,128)(2,1)S(1)} collective-permute-done((bf16[2,512,512]{2,1,0:T(8,128)(2,1)}, bf16[2,512,512]{2,1,0:T(8,128)(2,1)S(1)}, u32[]{:S(2)}, u32[]{:S(2)}) %collective-permute-start.5) | collective-permute-done | bytes 1048608 | tf_op jit(solution)/shard_map/ppermute | solution.py:508
  113.0 2.3 collective-permute-done.4.refs_0_.refs_1_
  119.4 35.9 %collective-permute-done.6 = bf16[512,512]{1,0:T(8,128)(2,1)} collective-permute-done((bf16[512,512]{1,0:T(8,128)(2,1)S(1)}, bf16[512,512]{1,0:T(8,128)(2,1)}, u32[]{:S(2)}, u32[]{:S(2)}) %collective-permute-start.6) | collective-permute-done | bytes 524320 | tf_op jit(solution)/shard_map/ppermute | solution.py:508
  157.2 10.2 %queries.1 = (bf16[1024,1024]{1,0:T(8,128)(2,1)}, f32[1024,1024]{1,0:T(8,128)}) custom-call(bf16[1024,1024]{1,0:T(8,128)(2,1)} %get-tuple-element.92.normed_ref, bf16[1024,2048]{1,0:T(8,128)(2,1)} %all-gather.3.cloned.1.call-done.w_ref, f32[1,128]{1,0:T(1,128)} %reshape.107.hgain_ref.qg_ref, f32[1024,128]{1,0:T(8,128)} %get-tuple-element.188.cos_ref, ...), custom_call_target="tpu_custom_call" | custom-call | flops 2147483648 | bytes 12582912 | tf_op jit(solution)/shard_map/queries/pallas_call | solution.py:45
  169.8 6.9 attend.5
  176.7 10.9 %attend.7 = (f32[512,1024]{1,0:T(8,128)}, f32[512,1024]{1,0:T(8,128)}) custom-call(s32[2]{0:T(128)} %pad_add_fusion.1.idx_ref, bf16[1024,1024]{1,0:T(8,128)(2,1)} %get-tuple-element.93.q_ref, s32[512,128]{1,0:T(8,128)} %broadcast_in_dim.67.lo_ref, bf16[2,512,512]{2,1,0:T(8,128)(2,1)} %get-tuple-element.94.refs_0_, ...), custom_call_target="tpu_custom_call" | custom-call | flops 5368709120 | bytes 8388608 | tf_op jit(solution)/shard_map/attend/pallas_call | solution.py:45
  190.7 9.4 %attend.6 = (bf16[1024,1024]{1,0:T(8,128)(2,1)}, f32[4,8,512]{2,1,0:T(8,128)}, bf16[512,1024]{1,0:T(8,128)(2,1)}) custom-call(s32[2]{0:T(128)} %pad_add_fusion.1.idx_ref, bf16[1024,1024]{1,0:T(8,128)(2,1)} %get-tuple-element.93.q_ref, s32[512,128]{1,0:T(8,128)} %broadcast_in_dim.67.lo_ref, bf16[2,512,512]{2,1,0:T(8,128)(2,1)} %collective-permute-done.4.refs_0_.refs_1_, ...), custom_call_target="tpu_custom_call" | custom-call | flops 6442450944 | bytes 8388608 | tf_op jit(solution)/shard_map/attend/pallas_call | solution.py:45
  200.2 13.9 %attend.8 = (f32[512,1024]{1,0:T(8,128)}, f32[512,1024]{1,0:T(8,128)}) custom-call(s32[2]{0:T(128)} %pad_add_fusion.1.idx_ref, bf16[1024,1024]{1,0:T(8,128)(2,1)} %get-tuple-element.93.q_ref, s32[512,128]{1,0:T(8,128)} %broadcast_in_dim.67.lo_ref, bf16[2,512,512]{2,1,0:T(8,128)(2,1)} %collective-permute-done.4.refs_0_.refs_1_, ...), custom_call_target="tpu_custom_call" | custom-call | flops 8589934592 | bytes 8388608 | tf_op jit(solution)/shard_map/attend/pallas_call | solution.py:45
  214.1 12.9 %attend.9 = (bf16[1024,1024]{1,0:T(8,128)(2,1)}, f32[4,8,512]{2,1,0:T(8,128)}, bf16[512,1024]{1,0:T(8,128)(2,1)}) custom-call(s32[2]{0:T(128)} %pad_add_fusion.1.idx_ref, bf16[1024,1024]{1,0:T(8,128)(2,1)} %get-tuple-element.93.q_ref, s32[512,128]{1,0:T(8,128)} %broadcast_in_dim.67.lo_ref, ...), custom_call_target="tpu_custom_call", output_to_operand_aliasing={{0}: (10, {})} | custom-call | flops 6442450944 | bytes 8388608 | tf_op jit(solution)/shard_map/attend/pallas_call | solution.py:45
  230.7 18.4 %feed_forward.2 = (f32[512,1024]{1,0:T(8,128)}, bf16[1024,1024]{1,0:T(8,128)(2,1)}, bf16[1024,1536]{1,0:T(8,128)(2,1)}, bf16[1024,3072]{1,0:T(8,128)(2,1)}, bf16...) custom-call(bf16[1024,1024]{1,0:T(8,128)(2,1)} %x_ref.11, bf16[512,1024]{1,0:T(8,128)(2,1)} %get-tuple-element.97.own_ref, ...), custom_call_target="tpu_custom_call" | custom-call | flops 9663676416 | bytes 20971520 | tf_op jit(solution)/shard_map/feed_forward/pallas_call | solution.py:45
  250.2 18.6 %feed_forward.3 = (f32[512,1024]{1,0:T(8,128)}, bf16[1024,1024]{1,0:T(8,128)(2,1)}, bf16[1024,1536]{1,0:T(8,128)(2,1)}, bf16[1024,3072]{1,0:T(8,128)(2,1)}, bf16...) custom-call(bf16[1024,1024]{1,0:T(8,128)(2,1)} %x_ref.11, ...), custom_call_target="tpu_custom_call", output_to_operand_aliasing={{1}: (7, {}), {2}: (8, {}), {3}: (9, {})} | custom-call | flops 9663676416 | bytes 20971520 | tf_op jit(solution)/shard_map/feed_forward/pallas_call | solution.py:45
  268.8 2.2 collective-permute-start.19
  271.0 9.7 %convolution_convert_fusion = bf16[1024,3072]{1,0:T(8,128)(2,1)S(1)} fusion(bf16[1024,1024]{1,0:T(8,128)(2,1)} %get-tuple-element.111, bf16[1024,3072]{1,0:T(8,128)(2,1)} %get-tuple-element.112), kind=kOutput, calls=%fused_computation.1 | convolution fusion | flops 6445596672 | bytes 14680064 | tf_op jit(solution)/shard_map/dot_general | solution.py:32
  280.8 3.7 fusion
  284.5 4.6 pad_maximum_fusion
  290.1 6.8 mixed_back.2
  297.9 6.8 mixed_back.3
  305.3 13.3 %attend_back.4 = (f32[512,1024]{1,0:T(8,128)}, bf16[2,512,512]{2,1,0:T(8,128)(2,1)}, bf16[2,512,512]{2,1,0:T(8,128)(2,1)}, bf16[2,512,512]{2,1,0:T(8,128)(2,1)},...) custom-call(s32[2]{0:T(128)} %pad_add_fusion.1.idx_ref, ...), custom_call_target="tpu_custom_call" | custom-call | flops 21474836480 | bytes 8388608 | tf_op jit(solution)/shard_map/attend_back/pallas_call | solution.py:45
  318.6 21.8 %attend_back.5 = (f32[512,1024]{1,0:T(8,128)}, bf16[2,512,512]{2,1,0:T(8,128)(2,1)}, bf16[2,512,512]{2,1,0:T(8,128)(2,1)}, bf16[2,512,512]{2,1,0:T(8,128)(2,1)},...) custom-call(s32[2]{0:T(128)} %pad_add_fusion.1.idx_ref, bf16[1024,1024]{1,0:T(8,128)(2,1)} %get-tuple-element.93.q_ref, ...), custom_call_target="tpu_custom_call" | custom-call | flops 18790481920 | bytes 8388608 | tf_op jit(solution)/shard_map/attend_back/pallas_call | solution.py:45
  340.4 17.5 %collective-permute-start.28 = (bf16[2,512,512]{2,1,0:T(8,128)(2,1)}, bf16[2,512,512]{2,1,0:T(8,128)(2,1)S(1)}, u32[]{:S(2)}, u32[]{:S(2)}) collective-permute-start(bf16[2,512,512]{2,1,0:T(8,128)(2,1)} %get-tuple-element.152), channel_id=1, source_target_pairs={{0,2},{2,0},{4,6},{6,4},{8,10},{10,8},{12,14},{14,12},{1,3},{3,1},... | collective-permute-start | bytes 3145736 | tf_op jit(solution)/shard_map/ppermute | solution.py:508
  357.9 25.6 %attend_back.6 = (f32[512,1024]{1,0:T(8,128)}, bf16[2,512,512]{2,1,0:T(8,128)(2,1)}, bf16[2,512,512]{2,1,0:T(8,128)(2,1)}, bf16[2,512,512]{2,1,0:T(8,128)(2,1)}, bf16[2,512,512]{2,1,0:T(8,128)(2,1)}) custom-call(s32[2]{0:T(128)} %pad_add_fusion.1.idx_ref, bf16[1024,1024]{1,0:T(8,128)(2,1)} %get-tuple-element.93.q_ref, ...), custom_call_target="tpu_custom_call" | custom-call | flops 21474836480 | bytes 8388608 | tf_op jit(solution)/shard_map/attend_back/pallas_call | solution.py:45
  384.2 15.7 %attend_back.7 = (f32[512,1024]{1,0:T(8,128)}, bf16[2,512,512]{2,1,0:T(8,128)(2,1)}, bf16[2,512,512]{2,1,0:T(8,128)(2,1)}) custom-call(s32[2]{0:T(128)} %pad_add_fusion.1.idx_ref, bf16[1024,1024]{1,0:T(8,128)(2,1)} %get-tuple-element.93.q_ref, bf16[512,1024]{1,0:T(8,128)(2,1)} %get-tuple-element.128.do_ref, f32[4,8,512]{2,1,0:T(8,128)} %get-tuple-element.129.lse_ref, ...), custom_call_target="tpu_custom_call" | custom-call | flops 10737418240 | bytes 8388608 | tf_op jit(solution)/shard_map/attend_back/pallas_call | solution.py:45
  400.3 3.7 convolution_convert_fusion.3
  409.1 28.2 %collective-permute-start.26 = (bf16[512,512]{1,0:T(8,128)(2,1)S(1)}, bf16[512,512]{1,0:T(8,128)(2,1)S(1)}, u32[]{:S(2)}, u32[]{:S(2)}) collective-permute-start(bf16[512,512]{1,0:T(8,128)(2,1)S(1)} %get-tuple-element.171), channel_id=1, source_target_pairs={{0,4},{2,6},{4,0},{6,2},{8,12},{10,14},{12,8},{14,10},{1,5},{3,7},... | collective-permute-start | bytes 1572872 | tf_op jit(solution)/shard_map/ppermute | solution.py:508
  437.4 28.9 %collective-permute-start.23 = (bf16[512,512]{1,0:T(8,128)(2,1)S(1)}, bf16[512,512]{1,0:T(8,128)(2,1)S(1)}, u32[]{:S(2)}, u32[]{:S(2)}) collective-permute-start(bf16[512,512]{1,0:T(8,128)(2,1)S(1)} %get-tuple-element.172), channel_id=1, source_target_pairs={{0,8},{2,10},{4,12},{6,14},{8,0},{10,2},{12,4},{14,6},{1,9},{3,11}... | collective-permute-start | bytes 1572872 | tf_op jit(solution)/shard_map/ppermute | solution.py:508
  468.2 6.0 collective-permute-done.26
  474.4 45.2 %collective-permute-start.27 = (bf16[2,512,512]{2,1,0:T(8,128)(2,1)S(1)}, bf16[2,512,512]{2,1,0:T(8,128)(2,1)S(1)}, u32[]{:S(2)}, u32[]{:S(2)}) collective-permute-start(bf16[2,512,512]{2,1,0:T(8,128)(2,1)S(1)} %pad_maximum_fusion.4), channel_id=1, source_target_pairs={{0,8},{2,10},{4,12},{6,14},{8,0},{10,2},{12,4},{14,6},{1,9},{3,11}... | collective-permute-start | bytes 3145736 | tf_op jit(solution)/shard_map/ppermute | solution.py:508
  522.0 14.7 %qkv_back.2 = (bf16[1024,2048]{1,0:T(8,128)(2,1)}, bf16[512,1024]{1,0:T(8,128)(2,1)}, f32[1,256]{1,0:T(1,128)}) custom-call(f32[512,1024]{1,0:T(8,128)} %get-tuple-element.149.dq_ref, f32[1024,1024]{1,0:T(8,128)} %get-tuple-element.124.ql_ref, f32[512,512]{1,0:T(8,128)} %get-tuple-element.150.kl_ref, f32[1,128]{1,0:T(1,128)} %reshape.107.hgain_ref.qg_ref, ...), custom_call_target="tpu_custom_call" | custom-call | flops 2147483648 | bytes 16777216 | tf_op jit(solution)/shard_map/qkv_back/pallas_call | solution.py:45
  536.6 6.6 collective-permute-done.27.refs_3_
  545.3 15.3 %qkv_back.3 = (bf16[1024,2048]{1,0:T(8,128)(2,1)}, bf16[512,1024]{1,0:T(8,128)(2,1)}, f32[1,256]{1,0:T(1,128)}) custom-call(f32[512,1024]{1,0:T(8,128)} %get-tuple-element.119.dq_ref, f32[1024,1024]{1,0:T(8,128)} %get-tuple-element.124.ql_ref, f32[512,512]{1,0:T(8,128)} %get-tuple-element.125.kl_ref, ...), custom_call_target="tpu_custom_call", output_to_operand_aliasing={{0}: (12, {})} | custom-call | flops 2147483648 | bytes 16777216 | tf_op jit(solution)/shard_map/qkv_back/pallas_call | solution.py:45
  560.6 8.3 %convolution_convert_fusion.2 = bf16[1024,2048]{1,0:T(8,128)(2,1)} fusion(bf16[1024,1024]{1,0:T(8,128)(2,1)S(1)} %copy-done.11, bf16[1024,2048]{1,0:T(8,128)(2,1)} %get-tuple-element.167), kind=kOutput, calls=%fused_computation.3 | convolution fusion | flops 4297064448 | bytes 10485760 | tf_op jit(solution)/shard_map/dot_general | solution.py:32
  575.3 30.6 %collective-permute-done.17 = bf16[512,1024]{1,0:T(8,128)(2,1)} collective-permute-done((bf16[512,1024]{1,0:T(8,128)(2,1)}, bf16[512,1024]{1,0:T(8,128)(2,1)}, u32[]{:S(2)}, u32[]{:S(2)}) %collective-permute-start.17) | collective-permute-done | bytes 1048608 | tf_op jit(solution)/shard_map/ppermute | solution.py:508
  608.1 30.5 %collective-permute-done.31.got_ref = bf16[512,1024]{1,0:T(8,128)(2,1)} collective-permute-done((bf16[512,1024]{1,0:T(8,128)(2,1)}, bf16[512,1024]{1,0:T(8,128)(2,1)}, u32[]{:S(2)}, u32[]{:S(2)}) %collective-permute-start.31) | collective-permute-done | bytes 1048608 | tf_op jit(solution)/shard_map/ppermute | solution.py:508
  638.6 4.8 tokens_back.2
  643.4 18.7 %collective-permute-done.30.got_ref = bf16[512,1024]{1,0:T(8,128)(2,1)} collective-permute-done((bf16[512,1024]{1,0:T(8,128)(2,1)}, bf16[512,1024]{1,0:T(8,128)(2,1)}, u32[]{:S(2)}, u32[]{:S(2)}) %collective-permute-start.30) | collective-permute-done | bytes 1048608 | tf_op jit(solution)/shard_map/ppermute | solution.py:508
  662.1 5.3 tokens_back.3
  668.2 13.7 %collective-permute-done.18 = bf16[512,1024]{1,0:T(8,128)(2,1)} collective-permute-done((bf16[512,1024]{1,0:T(8,128)(2,1)S(1)}, bf16[512,1024]{1,0:T(8,128)(2,1)}, u32[]{:S(2)}, u32[]{:S(2)}) %collective-permute-start.18) | collective-permute-done | bytes 1048608 | tf_op jit(solution)/shard_map/ppermute | solution.py:508
  685.4 11.2 %collective-permute-done.39 = f32[1,256]{1,0:T(1,128)S(1)} collective-permute-done((f32[1,256]{1,0:T(1,128)S(1)}, f32[1,256]{1,0:T(1,128)S(1)}, u32[]{:S(2)}, u32[]{:S(2)}) %collective-permute-start.39) | collective-permute-done | bytes 1056 | tf_op jit(solution)/shard_map/ppermute | solution.py:508
  696.7 3.6 collective-permute-done.40
  701.0 6.4 collective-permute-done.35
  712.9 52.3 %reduce-scatter.8.cloned.1.call-done = bf16[64,4608]{1,0:T(8,128)(2,1)} async-done(((bf16[1024,4608]{1,0:T(8,128)(2,1)}), bf16[64,4608]{1,0:T(8,128)(2,1)}) %reduce-scatter.8.cloned.1.call-update) | async-done | bytes 589840 | tf_op jit(solution)/shard_map/reduce_scatter | solution.py:681
  767.0 2.3 slice_reduce_fusion
  (231 shorter events, 79.1 us)
Async XLA Ops:
  7.2 61.5 %all-gather.3.cloned.1.call-start = ((), (), s32[]{:S(2)}) async-start(), calls=%async_computation.3 | async-start | bytes 4456448 | tf_op jit(solution)/shard_map/all_gather | solution.py:578
  9.0 181.7 %all-gather.5.cloned.1.call-start = ((), (), s32[]{:S(2)}) async-start(), calls=%async_computation.4 | async-start | bytes 12255232 | tf_op jit(solution)/shard_map/all_gather | solution.py:584
  16.9 691.2 %reduce-scatter.6.cloned.1.call-start = ((), (), s32[]{:S(2)}) async-start(), calls=%async_computation.6 | async-start | bytes 2228224 | tf_op jit(solution)/shard_map/reduce_scatter | solution.py:692
  17.1 1.3 collective-permute-start
  18.5 4.5 collective-permute-start.1
  23.0 4.0 collective-permute-start.2
  27.0 4.6 collective-permute-start.3
  74.4 37.3 %collective-permute-start.5 = (bf16[2,512,512]{2,1,0:T(8,128)(2,1)}, bf16[2,512,512]{2,1,0:T(8,128)(2,1)S(1)}, u32[]{:S(2)}, u32[]{:S(2)}) collective-permute-start(bf16[2,512,512]{2,1,0:T(8,128)(2,1)} %get-tuple-element.94.refs_0_), channel_id=1, source_target_pairs={{0,8},{2,10},{4,12},{6,14},{8,0},{10,2},{12,4},{14,6},{1,9},{3,11}... | collective-permute-start | bytes 3145736 | tf_op jit(solution)/shard_map/ppermute | solution.py:508
  75.9 39.4 %collective-permute-start.4 = (bf16[2,512,512]{2,1,0:T(8,128)(2,1)}, bf16[2,512,512]{2,1,0:T(8,128)(2,1)}, u32[]{:S(2)}, u32[]{:S(2)}) collective-permute-start(bf16[2,512,512]{2,1,0:T(8,128)(2,1)} %get-tuple-element.94.refs_0_), channel_id=1, source_target_pairs={{0,4},{2,6},{4,0},{6,2},{8,12},{10,14},{12,8},{14,10},{1,5},{3,7},... | collective-permute-start | bytes 3145736 | tf_op jit(solution)/shard_map/ppermute | solution.py:508
  83.2 84.3 %collective-permute-start.14 = (bf16[2,512,512]{2,1,0:T(8,128)(2,1)}, bf16[2,512,512]{2,1,0:T(8,128)(2,1)S(1)}, u32[]{:S(2)}, u32[]{:S(2)}) collective-permute-start(bf16[2,512,512]{2,1,0:T(8,128)(2,1)} %get-tuple-element.101.refs_2_), channel_id=1, source_target_pairs={{0,4},{2,6},{4,8},{6,10},{8,12},{10,14},{1,5},{3,7},{5,9},{7,11},{... | collective-permute-start | bytes 3145736 | tf_op jit(solution)/shard_map/ppermute | solution.py:513
  111.7 43.6 %collective-permute-start.6 = (bf16[512,512]{1,0:T(8,128)(2,1)S(1)}, bf16[512,512]{1,0:T(8,128)(2,1)}, u32[]{:S(2)}, u32[]{:S(2)}) collective-permute-start(bf16[512,512]{1,0:T(8,128)(2,1)S(1)} %slice_bitcast_fusion.5), channel_id=1, source_target_pairs={{0,4},{2,6},{4,0},{6,2},{8,12},{10,14},{12,8},{14,10},{1,5},{3,7},... | collective-permute-start | bytes 1572872 | tf_op jit(solution)/shard_map/ppermute | solution.py:508
  116.4 39.0 %collective-permute-start.7 = (bf16[512,512]{1,0:T(8,128)(2,1)S(1)}, bf16[512,512]{1,0:T(8,128)(2,1)}, u32[]{:S(2)}, u32[]{:S(2)}) collective-permute-start(bf16[512,512]{1,0:T(8,128)(2,1)S(1)} %slice_bitcast_fusion.4), channel_id=1, source_target_pairs={{0,8},{2,10},{4,12},{6,14},{8,0},{10,2},{12,4},{14,6},{1,9},{3,11}... | collective-permute-start | bytes 1572872 | tf_op jit(solution)/shard_map/ppermute | solution.py:508
  116.5 52.5 %collective-permute-start.11 = (bf16[2,512,512]{2,1,0:T(8,128)(2,1)}, bf16[2,512,512]{2,1,0:T(8,128)(2,1)}, u32[]{:S(2)}, u32[]{:S(2)}) collective-permute-start(bf16[2,512,512]{2,1,0:T(8,128)(2,1)} %get-tuple-element.94.refs_0_), channel_id=1, source_target_pairs={{0,2},{2,0},{4,6},{6,4},{8,10},{10,8},{12,14},{14,12},{1,3},{3,1},... | collective-permute-start | bytes 3145736 | tf_op jit(solution)/shard_map/ppermute | solution.py:508
  118.9 68.7 %collective-permute-start.8 = (bf16[2,512,512]{2,1,0:T(8,128)(2,1)}, bf16[2,512,512]{2,1,0:T(8,128)(2,1)S(1)}, u32[]{:S(2)}, u32[]{:S(2)}) collective-permute-start(bf16[2,512,512]{2,1,0:T(8,128)(2,1)} %collective-permute-done.4.refs_0_.refs_1_), channel_id=1, source_target_pairs={{0,2},{2,0},{4,6},{6,4},{8,10},{10,8},{12,14},{14,12},{1,3},{3,1},... | collective-permute-start | bytes 3145736 | tf_op jit(solution)/shard_map/ppermute | solution.py:508
  155.3 32.3 %collective-permute-start.9 = (bf16[2,512,512]{2,1,0:T(8,128)(2,1)S(1)}, bf16[2,512,512]{2,1,0:T(8,128)(2,1)S(1)}, u32[]{:S(2)}, u32[]{:S(2)}) collective-permute-start(bf16[2,512,512]{2,1,0:T(8,128)(2,1)S(1)} %collective-permute-done.5.refs_1_.refs_2_), channel_id=1, source_target_pairs={{0,2},{2,0},{4,6},{6,4},{8,10},{10,8},{12,14},{14,12},{1,3},{3,1},... | collective-permute-start | bytes 3145736 | tf_op jit(solution)/shard_map/ppermute | solution.py:508
  156.7 33.0 %collective-permute-start.10 = (bf16[2,512,512]{2,1,0:T(8,128)(2,1)S(1)}, bf16[2,512,512]{2,1,0:T(8,128)(2,1)S(1)}, u32[]{:S(2)}, u32[]{:S(2)}) collective-permute-start(bf16[2,512,512]{2,1,0:T(8,128)(2,1)S(1)} %pad_maximum_fusion.2.refs_2_.refs_0_.refs_4_), channel_id=1, source_target_pairs={{0,2},{2,0},{4,6},{6,4},{8,10},{10,8},{12,14},{14,12},{1,3},{3,1},... | collective-permute-start | bytes 3145736 | tf_op jit(solution)/shard_map/ppermute | solution.py:508
  168.7 45.3 %collective-permute-start.15 = (bf16[2,512,512]{2,1,0:T(8,128)(2,1)}, bf16[2,512,512]{2,1,0:T(8,128)(2,1)}, u32[]{:S(2)}, u32[]{:S(2)}) collective-permute-start(bf16[2,512,512]{2,1,0:T(8,128)(2,1)} %broadcast_select_fusion.1), channel_id=1, source_target_pairs={{0,2},{2,0},{4,6},{6,4},{8,10},{10,8},{12,14},{14,12},{1,3},{3,1},... | collective-permute-start | bytes 3145736 | tf_op jit(solution)/shard_map/ppermute | solution.py:508
  200.1 29.6 %collective-permute-start.12 = (bf16[512,1024]{1,0:T(8,128)(2,1)}, bf16[512,1024]{1,0:T(8,128)(2,1)S(1)}, u32[]{:S(2)}, u32[]{:S(2)}) collective-permute-start(bf16[512,1024]{1,0:T(8,128)(2,1)} %get-tuple-element.97.own_ref), channel_id=1, source_target_pairs={{0,1},{1,0},{2,3},{3,2},{4,5},{5,4},{6,7},{7,6},{8,9},{9,8},{10,11... | collective-permute-start | bytes 3145736 | tf_op jit(solution)/shard_map/ppermute | solution.py:508
  226.9 22.2 %collective-permute-start.16 = (bf16[512,1024]{1,0:T(8,128)(2,1)}, bf16[512,1024]{1,0:T(8,128)(2,1)S(1)}, u32[]{:S(2)}, u32[]{:S(2)}) collective-permute-start(bf16[512,1024]{1,0:T(8,128)(2,1)} %get-tuple-element.107.own_ref), channel_id=1, source_target_pairs={{0,1},{1,0},{2,3},{3,2},{4,5},{5,4},{6,7},{7,6},{8,9},{9,8},{10,11... | collective-permute-start | bytes 3145736 | tf_op jit(solution)/shard_map/ppermute | solution.py:508
  249.1 40.0 %collective-permute-start.13 = (bf16[512,1024]{1,0:T(8,128)(2,1)}, bf16[512,1024]{1,0:T(8,128)(2,1)S(1)}, u32[]{:S(2)}, u32[]{:S(2)}) collective-permute-start(bf16[512,1024]{1,0:T(8,128)(2,1)} %get-tuple-element.100.own_ref), channel_id=1, source_target_pairs={{0,1},{1,0},{2,3},{3,2},{4,5},{5,4},{6,7},{7,6},{8,9},{9,8},{10,11... | collective-permute-start | bytes 3145736 | tf_op jit(solution)/shard_map/ppermute | solution.py:508
  268.8 28.1 %collective-permute-start.19 = (bf16[512,1024]{1,0:T(8,128)(2,1)}, bf16[512,1024]{1,0:T(8,128)(2,1)S(1)}, u32[]{:S(2)}, u32[]{:S(2)}) collective-permute-start(bf16[512,1024]{1,0:T(8,128)(2,1)} %get-tuple-element.126.own_ref), channel_id=1, source_target_pairs={{0,1},{1,0},{2,3},{3,2},{4,5},{5,4},{6,7},{7,6},{8,9},{9,8},{10,11... | collective-permute-start | bytes 3145736 | tf_op jit(solution)/shard_map/ppermute | solution.py:508
  340.4 63.7 %collective-permute-start.28 = (bf16[2,512,512]{2,1,0:T(8,128)(2,1)}, bf16[2,512,512]{2,1,0:T(8,128)(2,1)S(1)}, u32[]{:S(2)}, u32[]{:S(2)}) collective-permute-start(bf16[2,512,512]{2,1,0:T(8,128)(2,1)} %get-tuple-element.152), channel_id=1, source_target_pairs={{0,2},{2,0},{4,6},{6,4},{8,10},{10,8},{12,14},{14,12},{1,3},{3,1},... | collective-permute-start | bytes 3145736 | tf_op jit(solution)/shard_map/ppermute | solution.py:508
  383.5 53.8 %collective-permute-start.25 = (bf16[2,512,512]{2,1,0:T(8,128)(2,1)}, bf16[2,512,512]{2,1,0:T(8,128)(2,1)S(1)}, u32[]{:S(2)}, u32[]{:S(2)}) collective-permute-start(bf16[2,512,512]{2,1,0:T(8,128)(2,1)} %get-tuple-element.148), channel_id=1, source_target_pairs={{0,2},{2,0},{4,6},{6,4},{8,10},{10,8},{12,14},{14,12},{1,3},{3,1},... | collective-permute-start | bytes 3145736 | tf_op jit(solution)/shard_map/ppermute | solution.py:508
  383.6 23.8 %collective-permute-start.22 = (bf16[2,512,512]{2,1,0:T(8,128)(2,1)}, bf16[2,512,512]{2,1,0:T(8,128)(2,1)}, u32[]{:S(2)}, u32[]{:S(2)}) collective-permute-start(bf16[2,512,512]{2,1,0:T(8,128)(2,1)} %get-tuple-element.146), channel_id=1, source_target_pairs={{0,2},{2,0},{4,6},{6,4},{8,10},{10,8},{12,14},{14,12},{1,3},{3,1},... | collective-permute-start | bytes 3145736 | tf_op jit(solution)/shard_map/ppermute | solution.py:508
  384.1 82.5 %collective-permute-start.21 = (bf16[2,512,512]{2,1,0:T(8,128)(2,1)}, bf16[2,512,512]{2,1,0:T(8,128)(2,1)}, u32[]{:S(2)}, u32[]{:S(2)}) collective-permute-start(bf16[2,512,512]{2,1,0:T(8,128)(2,1)} %get-tuple-element.144), channel_id=1, source_target_pairs={{0,2},{2,0},{4,6},{6,4},{8,10},{10,8},{12,14},{14,12},{1,3},{3,1},... | collective-permute-start | bytes 3145736 | tf_op jit(solution)/shard_map/ppermute | solution.py:508
  399.9 136.8 %collective-permute-start.20 = (bf16[2,512,512]{2,1,0:T(8,128)(2,1)}, bf16[2,512,512]{2,1,0:T(8,128)(2,1)}, u32[]{:S(2)}, u32[]{:S(2)}) collective-permute-start(bf16[2,512,512]{2,1,0:T(8,128)(2,1)} %get-tuple-element.142), channel_id=1, source_target_pairs={{0,2},{2,0},{4,6},{6,4},{8,10},{10,8},{12,14},{14,12},{1,3},{3,1},... | collective-permute-start | bytes 3145736 | tf_op jit(solution)/shard_map/ppermute | solution.py:508
  404.0 305.6 %reduce-scatter.4.cloned.1.call-start = ((), (), s32[]{:S(2)}) async-start(), calls=%async_computation.5 | async-start | bytes 4456448 | tf_op jit(solution)/shard_map/reduce_scatter | solution.py:724
  405.7 115.3 %collective-permute-start.29 = (bf16[2,512,512]{2,1,0:T(8,128)(2,1)S(1)}, bf16[2,512,512]{2,1,0:T(8,128)(2,1)S(1)}, u32[]{:S(2)}, u32[]{:S(2)}) collective-permute-start(bf16[2,512,512]{2,1,0:T(8,128)(2,1)S(1)} %add_convert_fusion), channel_id=1, source_target_pairs={{4,0},{6,2},{8,4},{10,6},{12,8},{14,10},{5,1},{7,3},{9,5},{11,7},{... | collective-permute-start | bytes 3145736 | tf_op jit(solution)/shard_map/ppermute | solution.py:513
  407.4 58.9 %copy-start.14 = (bf16[2,512,512]{2,1,0:T(8,128)(2,1)S(1)}, bf16[2,512,512]{2,1,0:T(8,128)(2,1)}, u32[]{:S(2)}) copy-start(bf16[2,512,512]{2,1,0:T(8,128)(2,1)} %get-tuple-element.147) | copy-start | bytes 3145732
  409.1 57.5 %copy-start.13 = (bf16[2,512,512]{2,1,0:T(8,128)(2,1)S(1)}, bf16[2,512,512]{2,1,0:T(8,128)(2,1)}, u32[]{:S(2)}) copy-start(bf16[2,512,512]{2,1,0:T(8,128)(2,1)} %get-tuple-element.143) | copy-start | bytes 3145732
  409.1 65.0 %collective-permute-start.26 = (bf16[512,512]{1,0:T(8,128)(2,1)S(1)}, bf16[512,512]{1,0:T(8,128)(2,1)S(1)}, u32[]{:S(2)}, u32[]{:S(2)}) collective-permute-start(bf16[512,512]{1,0:T(8,128)(2,1)S(1)} %get-tuple-element.171), channel_id=1, source_target_pairs={{0,4},{2,6},{4,0},{6,2},{8,12},{10,14},{12,8},{14,10},{1,5},{3,7},... | collective-permute-start | bytes 1572872 | tf_op jit(solution)/shard_map/ppermute | solution.py:508
  437.4 82.2 %collective-permute-start.23 = (bf16[512,512]{1,0:T(8,128)(2,1)S(1)}, bf16[512,512]{1,0:T(8,128)(2,1)S(1)}, u32[]{:S(2)}, u32[]{:S(2)}) collective-permute-start(bf16[512,512]{1,0:T(8,128)(2,1)S(1)} %get-tuple-element.172), channel_id=1, source_target_pairs={{0,8},{2,10},{4,12},{6,14},{8,0},{10,2},{12,4},{14,6},{1,9},{3,11}... | collective-permute-start | bytes 1572872 | tf_op jit(solution)/shard_map/ppermute | solution.py:508
  474.4 68.8 %collective-permute-start.27 = (bf16[2,512,512]{2,1,0:T(8,128)(2,1)S(1)}, bf16[2,512,512]{2,1,0:T(8,128)(2,1)S(1)}, u32[]{:S(2)}, u32[]{:S(2)}) collective-permute-start(bf16[2,512,512]{2,1,0:T(8,128)(2,1)S(1)} %pad_maximum_fusion.4), channel_id=1, source_target_pairs={{0,8},{2,10},{4,12},{6,14},{8,0},{10,2},{12,4},{14,6},{1,9},{3,11}... | collective-permute-start | bytes 3145736 | tf_op jit(solution)/shard_map/ppermute | solution.py:508
  519.9 24.4 %collective-permute-start.24 = (bf16[2,512,512]{2,1,0:T(8,128)(2,1)S(1)}, bf16[2,512,512]{2,1,0:T(8,128)(2,1)S(1)}, u32[]{:S(2)}, u32[]{:S(2)}) collective-permute-start(bf16[2,512,512]{2,1,0:T(8,128)(2,1)S(1)} %pad_maximum_fusion.3), channel_id=1, source_target_pairs={{0,4},{2,6},{4,0},{6,2},{8,12},{10,14},{12,8},{14,10},{1,5},{3,7},... | collective-permute-start | bytes 3145736 | tf_op jit(solution)/shard_map/ppermute | solution.py:508
  569.0 196.2 %reduce-scatter.8.cloned.1.call-start = ((), (), s32[]{:S(2)}) async-start(), calls=%async_computation.7 | async-start | bytes 10027008 | tf_op jit(solution)/shard_map/reduce_scatter | solution.py:681
  569.6 36.3 %collective-permute-start.17 = (bf16[512,1024]{1,0:T(8,128)(2,1)}, bf16[512,1024]{1,0:T(8,128)(2,1)}, u32[]{:S(2)}, u32[]{:S(2)}) collective-permute-start(bf16[512,1024]{1,0:T(8,128)(2,1)} %get-tuple-element.120), channel_id=1, source_target_pairs={{0,1},{1,0},{2,3},{3,2},{4,5},{5,4},{6,7},{7,6},{8,9},{9,8},{10,11... | collective-permute-start | bytes 3145736 | tf_op jit(solution)/shard_map/ppermute | solution.py:508
  569.7 68.9 %collective-permute-start.31 = (bf16[512,1024]{1,0:T(8,128)(2,1)}, bf16[512,1024]{1,0:T(8,128)(2,1)}, u32[]{:S(2)}, u32[]{:S(2)}) collective-permute-start(bf16[512,1024]{1,0:T(8,128)(2,1)} %get-tuple-element.157.own_ref), channel_id=1, source_target_pairs={{0,1},{1,0},{2,3},{3,2},{4,5},{5,4},{6,7},{7,6},{8,9},{9,8},{10,11... | collective-permute-start | bytes 3145736 | tf_op jit(solution)/shard_map/ppermute | solution.py:508
  571.7 90.4 %collective-permute-start.30 = (bf16[512,1024]{1,0:T(8,128)(2,1)}, bf16[512,1024]{1,0:T(8,128)(2,1)}, u32[]{:S(2)}, u32[]{:S(2)}) collective-permute-start(bf16[512,1024]{1,0:T(8,128)(2,1)} %get-tuple-element.155.own_ref), channel_id=1, source_target_pairs={{0,1},{1,0},{2,3},{3,2},{4,5},{5,4},{6,7},{7,6},{8,9},{9,8},{10,11... | collective-permute-start | bytes 3145736 | tf_op jit(solution)/shard_map/ppermute | solution.py:508
  571.8 110.1 %collective-permute-start.18 = (bf16[512,1024]{1,0:T(8,128)(2,1)S(1)}, bf16[512,1024]{1,0:T(8,128)(2,1)}, u32[]{:S(2)}, u32[]{:S(2)}) collective-permute-start(bf16[512,1024]{1,0:T(8,128)(2,1)S(1)} %copy-done.12), channel_id=1, source_target_pairs={{0,1},{1,0},{2,3},{3,2},{4,5},{5,4},{6,7},{7,6},{8,9},{9,8},{10,11... | collective-permute-start | bytes 3145736 | tf_op jit(solution)/shard_map/ppermute | solution.py:508
  573.7 1.2 collective-permute-start.36
  574.9 33.0 %collective-permute-start.37 = (f32[1,256]{1,0:T(1,128)S(1)}, f32[1,256]{1,0:T(1,128)S(1)}, u32[]{:S(2)}, u32[]{:S(2)}) collective-permute-start(f32[1,256]{1,0:T(1,128)S(1)} %add.149), channel_id=1, source_target_pairs={{0,4},{2,6},{4,0},{6,2},{8,12},{10,14},{12,8},{14,10},{1,5},{3,7},... | collective-permute-start | bytes 3080 | tf_op jit(solution)/shard_map/ppermute | solution.py:508
  608.0 75.6 %collective-permute-start.38 = (f32[1,256]{1,0:T(1,128)S(1)}, f32[1,256]{1,0:T(1,128)S(1)}, u32[]{:S(2)}, u32[]{:S(2)}) collective-permute-start(f32[1,256]{1,0:T(1,128)S(1)} %add.150), channel_id=1, source_target_pairs={{0,8},{2,10},{4,12},{6,14},{8,0},{10,2},{12,4},{14,6},{1,9},{3,11}... | collective-permute-start | bytes 3080 | tf_op jit(solution)/shard_map/ppermute | solution.py:508
  668.1 15.6 %collective-permute-start.32 = (f32[2,1024]{1,0:T(2,128)S(1)}, f32[2,1024]{1,0:T(2,128)S(1)}, u32[]{:S(2)}, u32[]{:S(2)}) collective-permute-start(f32[2,1024]{1,0:T(2,128)S(1)} %pad_maximum_fusion.8), channel_id=1, source_target_pairs={{0,2},{2,0},{4,6},{6,4},{8,10},{10,8},{12,14},{14,12},{1,3},{3,1},... | collective-permute-start | bytes 24584 | tf_op jit(solution)/shard_map/ppermute | solution.py:508
  683.7 12.9 %collective-permute-start.39 = (f32[1,256]{1,0:T(1,128)S(1)}, f32[1,256]{1,0:T(1,128)S(1)}, u32[]{:S(2)}, u32[]{:S(2)}) collective-permute-start(f32[1,256]{1,0:T(1,128)S(1)} %add.151), channel_id=1, source_target_pairs={{0,16},{16,0},{1,17},{17,1},{2,18},{18,2},{3,19},{19,3},{4,20},{20... | collective-permute-start | bytes 3080 | tf_op jit(solution)/shard_map/ppermute | solution.py:508
  683.8 12.8 %collective-permute-start.33 = (f32[2,1024]{1,0:T(2,128)S(1)}, f32[2,1024]{1,0:T(2,128)S(1)}, u32[]{:S(2)}, u32[]{:S(2)}) collective-permute-start(f32[2,1024]{1,0:T(2,128)S(1)} %fusion.12), channel_id=1, source_target_pairs={{0,4},{2,6},{4,0},{6,2},{8,12},{10,14},{12,8},{14,10},{1,5},{3,7},... | collective-permute-start | bytes 24584 | tf_op jit(solution)/shard_map/ppermute | solution.py:508
  696.6 3.7 collective-permute-start.40
  696.6 3.7 collective-permute-start.34
  700.4 7.0 collective-permute-start.35
  (35 other events, 294.2 us)
Sparse Core Ops, SparseCore 0:
  11.0 57.7 all-gather.2
  71.1 119.5 all-gather.4
  404.2 118.8 reduce-scatter.5
  569.1 74.3 reduce-scatter.3
  648.1 117.1 reduce-scatter.7
